TPU v7x, 128 devices: a whole 4x4x4 slice. The times are simulated.
128 devices in a mesh: ang: 64 (over y_lo, x, z, core), row: 2 (over y_hi).
Axes of the slice: x: 4, y: 4 (y_hi: 2, y_lo: 2; y = y_hi * 2 + y_lo), z: 4, core: 2. Of those that a mesh axis runs over, the one named last changes fastest.
Arguments:
- projections: float32 [128, 128, 4096], P('ang', 'row'), may hold values from 0.05 to 1
- correlation: int32 [128], P('ang'), may hold values from 128 to 512
- offset: int32 [128], P('ang'), may hold values from 0 to 127
- smooth_taps: float32 [2, 33], replicated, may hold values from 0.2 to 1
Outputs:
- sinograms: float32 [2, 64, 128, 8192], P('row', 'ang')
Inputs may be any that keep to these rules, and one draw needn't show every extreme that they name: Every offset is smaller than every correlation; correlations are at least 1.
All inputs are finite; a program needn't handle non-finite values.
Results may differ from a plain program's by a relative error of at most 0.0003.
Values sent between devices are 32-bit elements; how exact they have to be, the bound alone decides.
No kernel may reach another device: no remote copies, remote signals or barrier semaphores. Data moves between devices by JAX's collectives and lax.ppermute only.
A program may use at most 128 MiB of HBM per device.

v0:
```python
import functools
import math

import jax
import jax.numpy as jnp
import numpy as np
from jax import lax
from jax.experimental import pallas as pl
from jax.experimental.pallas import tpu as pltpu

ANGLE_TAPS = 31
LANES = 128
OUTER = 64
BLOCKS = 36
LEFT = 4
REACH = 16
TAPS = 2 * REACH + 1
LENGTH = OUTER * LANES
MIN_OVERLAP_OFFSET = 127
f32, bf16 = jnp.float32, jnp.bfloat16


def halves(x):
    high = x.astype(bf16)
    return high, (x - high.astype(f32)).astype(bf16)


def thirds(x):
    high = x.astype(bf16)
    rest = x - high.astype(f32)
    middle = rest.astype(bf16)
    return high, middle, (rest - middle.astype(f32)).astype(bf16)


def mxu(a, b):
    return jnp.dot(a, b, preferred_element_type=f32)


def source_kernel(ints, taps, own, halo, seam, seam_halo, out):
    rows = own.shape[1]
    halo_rows = halo.shape[1]
    every = rows + halo_rows
    width_blocks = own.shape[2] // LANES
    width = own.shape[2]
    row_group = ints[4]
    lane = lax.broadcasted_iota(jnp.int32, (1, LANES), 1)

    target = lax.broadcasted_iota(jnp.int32, (rows, 3 * every), 0)
    place = lax.broadcasted_iota(jnp.int32, (rows, 3 * every), 1)
    third = place // every
    source = place - third * every
    source = jnp.where((source >= rows) & (row_group > 0), source - every, source)
    tap_at = source - target + REACH
    matrix = jnp.zeros((rows, 3 * every), f32)
    for t in range(TAPS):
        matrix = jnp.where(tap_at == t, taps[1, t], matrix)
    m_high, m_mid, m_low = thirds(matrix)
    left_one = jnp.where(third == 1, m_mid.astype(f32), m_high.astype(f32)).astype(bf16)
    left_two = jnp.where(
        third == 0, m_low.astype(f32), jnp.where(third == 1, m_mid.astype(f32), m_high.astype(f32))
    ).astype(bf16)

    def smooth(pair):
        high, mid, low = thirds(pair)
        one = jnp.concatenate([high, high, mid], axis=0)
        two = jnp.concatenate([high, mid, low], axis=0)
        return mxu(left_one, one) + mxu(left_two, two)

    for s in range(2):
        overlap, lead = ints[s], ints[2 + s]
        shift = overlap - lead
        skip = shift // LANES
        turn = shift - skip * LANES
        back = lax.rem(LANES - turn, LANES)
        keep = lane < LANES - turn

        def turned(block, s=s, back=back):
            at = pl.multiple_of(jnp.clip(block, 0, width_blocks - 1) * LANES, LANES)
            both = jnp.concatenate([own[s, :, pl.ds(at, LANES)], halo[s, :, pl.ds(at, LANES)]], axis=0)
            return pltpu.roll(both, back, 1)

        def store(b, value, s=s):
            for g in range(rows // 8):
                out[pl.ds(8 * g * 2 * BLOCKS + s * BLOCKS + LEFT + b, 8, stride=2 * BLOCKS), :] = value[8 * g : 8 * g + 8]

        def finish(b, first, second, store=store):
            value = smooth(jnp.concatenate([first, second], axis=1))
            store(b, value[:, :LANES])
            return value[:, LANES:]

        mirror = (lead - 1 - lane) & (LANES - 1)
        mirror = jnp.broadcast_to(mirror, (every, LANES))
        flipped = []
        for j in range(LEFT):
            both = jnp.concatenate(
                [seam[s, :, LANES * j : LANES * (j + 1)], seam_halo[s, :, LANES * j : LANES * (j + 1)]], axis=0
            )
            flipped.append(jnp.take_along_axis(both, mirror, axis=1, mode="promise_in_bounds"))

        def blended(b, first, second):
            u = LANES * b + shift + lane
            weight = jnp.clip((u.astype(f32) + 0.5) / overlap.astype(f32), 0.0, 1.0)
            mine = jnp.where(keep, first, second)
            other = jnp.where(lane < lead, flipped[min(max(-b, 0), 3)], flipped[min(max(-b - 1, 0), 3)])
            return -jnp.log(weight * mine + (1.0 - weight) * other)

        for b in range(-LEFT, 2, 2):
            parts = [turned(b + skip + i) for i in range(3)]
            store(b + 1, finish(b, blended(b, parts[0], parts[1]), blended(b + 1, parts[1], parts[2])))

        def plain(b, first, second):
            u = LANES * b + shift + lane
            return -jnp.log(jnp.where(u < width, jnp.where(keep, first, second), 1.0))

        def pair(i, carry):
            b = 2 * i
            parts = [turned(b + skip + j) for j in range(3)]
            value = finish(b, plain(b, parts[0], parts[1]), plain(b + 1, parts[1], parts[2]))
            last = b + 1 == width_blocks - 1
            value = jnp.where(last & (lane == LANES - 1), shift.astype(f32), value)
            value = jnp.where(last & (lane == LANES - 2) & (shift > 1), lead.astype(f32), value)
            store(b + 1, value)
            return carry

        lax.fori_loop(1, width_blocks // 2, pair, 0)


def times(a, b):
    return (a[0] * b[0] - a[1] * b[1], a[0] * b[1] + a[1] * b[0])


def dft(x, sign):
    n = len(x)
    if n == 1:
        return x
    even, odd = dft(x[0::2], sign), dft(x[1::2], sign)
    root = math.sqrt(0.5)
    first, second = [], []
    for k in range(n // 2):
        re, im = odd[k]
        if 4 * k == n:
            re, im = -sign * im, sign * re
        elif 8 * k == n:
            re, im = root * (re - sign * im), root * (im + sign * re)
        elif 8 * k == 3 * n:
            re, im = root * (-re - sign * im), root * (-im + sign * re)
        first.append((even[k][0] + re, even[k][1] + im))
        second.append((even[k][0] - re, even[k][1] - im))
    return first + second


def small_twist(value, power, sign):
    if power % OUTER == 0:
        return value
    angle = sign * 2.0 * math.pi * (power % OUTER) / OUTER
    return times(value, (np.float32(math.cos(angle)), np.float32(math.sin(angle))))


def sinogram_kernel(
    x, gain_re, gain_im, ramp, ends, twist_re, twist_im, end_u, end_v, box, forward, backward, end_w,
    out, field, mid_re, mid_im, rows, end_rows,
):
    half = out.shape[0] // 2
    lane = lax.broadcasted_iota(jnp.int32, (8, LANES), 1)

    def place(g, carry):
        sides = []
        for side in range(2):
            start = (side * half + 8 * g) * BLOCKS
            blocks = [x[pl.ds(start + k, 8, stride=BLOCKS), :] for k in range(BLOCKS)]
            last = blocks[-1]
            shift = last[:, LANES - 1 :]
            lead = jnp.where(shift > 1.5, last[:, LANES - 2 : LANES - 1], float(MIN_OVERLAP_OFFSET))
            hidden = (lane == LANES - 1) | ((lane == LANES - 2) & (shift > 1.5))
            blocks[-1] = jnp.where(hidden, 0.0, last)
            sides.append((blocks, shift.astype(jnp.int32), lead.astype(jnp.int32)))
        for side in range(2):
            mine, _, lead = sides[side]
            theirs, their_shift, _ = sides[1 - side]
            at = pl.ds(pl.multiple_of(side * half + 8 * g, 8), 8)
            spot = LANES - 1 + lead - their_shift - lane
            index = spot & (LANES - 1)
            jump = (spot >> 7) + 4
            mirrored = {}
            for k in range(OUTER // 2):
                mirrored[k] = jnp.take_along_axis(theirs[LEFT + k], index, axis=1, mode="promise_in_bounds")
            mirrored[-1] = mirrored[0]
            mirrored[OUTER // 2] = jnp.zeros((8, LANES), f32)
            for step in (1, 2, 4):
                moved = (jump & step) != 0
                top = OUTER // 2
                mirrored = {
                    k: jnp.where(moved, mirrored[min(k + step, top)], mirrored[k]) for k in mirrored
                }
            for c in range(OUTER // 2 - LEFT + 1):
                value = mirrored[OUTER // 2 - 5 - c]
                if c == OUTER // 2 - LEFT:
                    value = jnp.where(lane >= lead, mine[0], value)
                field[c, at, :] = value
            for k in range(1, BLOCKS):
                field[OUTER // 2 - LEFT + k, at, :] = mine[k]
        return carry

    lax.fori_loop(0, half // 8, place, 0)

    def highpass(i, carry):
        both = jnp.concatenate([field[2 * i], field[2 * i + 1]], axis=1)
        high, low = halves(both)
        sums = mxu(box[...], jnp.concatenate([high, low], axis=0))
        both = both - sums * np.float32(1.0 / ANGLE_TAPS)
        field[2 * i] = both[:, :LANES]
        field[2 * i + 1] = both[:, LANES:]
        return carry

    lax.fori_loop(0, OUTER // 2, highpass, 0)

    border = jnp.concatenate(
        [field[0, :half], field[0, half:], field[OUTER - 1, :half], field[OUTER - 1, half:]], axis=1
    )
    end_rows[...] = jnp.dot(border, ends[...], precision=lax.Precision.HIGHEST, preferred_element_type=f32)

    def filtered(g, carry):
        low_at = pl.ds(pl.multiple_of(8 * g, 8), 8)
        high_at = pl.ds(pl.multiple_of(half + 8 * g, 8), 8)
        for b in range(8):
            got = dft([(field[8 * a + b, low_at, :], field[8 * a + b, high_at, :]) for a in range(8)], -1.0)
            for d in range(8):
                mid_re[8 * d + b], mid_im[8 * d + b] = small_twist(got[d], d * b, -1.0)
        for d in range(8):
            got = dft([(mid_re[8 * d + b], mid_im[8 * d + b]) for b in range(8)], -1.0)
            for e in range(8):
                k = d + 8 * e
                re, im = times(got[e], (twist_re[k : k + 1, :], twist_im[k : k + 1, :]))
                rows[k, :, :LANES] = re
                rows[k, :, LANES:] = im
        for part in range(2):
            n = OUTER // 2
            span = slice(part * n, (part + 1) * n)
            high, low = halves(rows[span].reshape(n * 8, 2 * LANES))
            spectrum = mxu(high, forward[0]) + mxu(low, forward[0]) + mxu(high, forward[1])
            spectrum = spectrum.reshape(n, 8, 2 * LANES)
            here = end_rows[low_at, :]
            tail = here[None, :, :LANES] * end_u[span][:, None, :] + here[None, :, LANES:] * end_v[span][:, None, :]
            tail = tail.reshape(n * 8, LANES)
            t_high = tail.astype(bf16).astype(f32)
            front = lax.broadcasted_iota(jnp.int32, (1, LANES), 1) < LANES // 2
            t_one = jnp.where(front, t_high, tail - t_high).astype(bf16)
            t_two = jnp.where(front, t_high, 0.0).astype(bf16)
            wrapped = mxu(jnp.concatenate([t_one, t_two], axis=1), end_w[...]).reshape(n, 8, 2 * LANES)
            g_re, g_im, r = gain_re[span][:, None, :], gain_im[span][:, None, :], ramp[span][:, None, :]
            re, im = times((spectrum[..., :LANES], spectrum[..., LANES:]), (g_re, g_im))
            re = re - r * wrapped[..., :LANES]
            im = im - r * wrapped[..., LANES:]
            high, low = halves(jnp.concatenate([re, im], axis=2).reshape(n * 8, 2 * LANES))
            signal = mxu(high, backward[0]) + mxu(low, backward[0]) + mxu(high, backward[1])
            signal = signal.reshape(n, 8, 2 * LANES)
            re, im = times(
                (signal[..., :LANES], signal[..., LANES:]), (twist_re[span][:, None, :], -twist_im[span][:, None, :])
            )
            rows[span, :, :LANES] = re
            rows[span, :, LANES:] = im
        for d in range(8):
            got = dft([(rows[d + 8 * e, :, :LANES], rows[d + 8 * e, :, LANES:]) for e in range(8)], 1.0)
            for b in range(8):
                mid_re[8 * d + b], mid_im[8 * d + b] = small_twist(got[b], d * b, 1.0)
        for b in range(8):
            got = dft([(mid_re[8 * d + b], mid_im[8 * d + b]) for d in range(8)], 1.0)
            for a in range(8):
                c = 8 * a + b
                out[low_at, c * LANES : (c + 1) * LANES] = got[a][0]
                out[high_at, c * LANES : (c + 1) * LANES] = got[a][1]
        return carry

    lax.fori_loop(0, half // 8, filtered, 0)


@functools.lru_cache(maxsize=None)
def tables(nproj):
    k1 = np.arange(OUTER)[:, None]
    l = np.arange(LANES)[None, :]
    angle = 2.0 * np.pi * (k1 * l % LENGTH) / LENGTH
    table = dict(twist_re=np.cos(angle), twist_im=-np.sin(angle))
    inner = 2.0 * np.pi * (np.arange(LANES)[:, None] * l % LANES) / LANES
    cos, sin = np.cos(inner), np.sin(inner)
    forward = np.block([[cos, -sin], [sin, cos]])
    backward = np.block([[cos, sin], [-sin, cos]])

    def two(w):
        high = w.astype(np.float32).astype(jnp.bfloat16)
        low = (w - high.astype(np.float64)).astype(np.float32).astype(jnp.bfloat16)
        return high, low

    table["forward"] = np.stack(two(forward))
    table["backward"] = np.stack(two(backward))
    columns = np.concatenate([np.arange(REACH), LENGTH - REACH + np.arange(REACH)])
    some = columns % LANES
    end_w = np.concatenate([forward[some], forward[LANES + some]], axis=0)
    high, low = two(end_w)
    table["end_w"] = np.concatenate([high, high, low, np.zeros_like(low)], axis=0)
    theta = 2.0 * np.pi * (k1 * columns[None, :] % LENGTH) / LENGTH
    table["end_u"] = np.tile(np.cos(theta), (1, 4))
    table["end_v"] = np.tile(np.concatenate([np.sin(theta), -np.sin(theta)], axis=1), (1, 2))
    tap_at = np.full((4, LANES, 2, 4, 2 * REACH), -1, np.int32)
    for i in range(REACH):
        for arrangement in range(2):
            for group in range(4):
                part = (group + arrangement) % 2
                for t in range(TAPS):
                    if LANES - REACH + i + t < LANES:
                        tap_at[2 + part, LANES - REACH + i + t, arrangement, group, i] = t
                    if i + t - 2 * REACH >= 0:
                        tap_at[part, i + t - 2 * REACH, arrangement, group, REACH + i] = t
    table["tap_at"] = tap_at.reshape(4 * LANES, 2 * LANES)
    frequency = k1 + OUTER * l
    table["ramp"] = np.minimum(frequency, LENGTH - frequency) / (LENGTH / 2) / LENGTH
    lag = np.arange(TAPS) - REACH
    a = 2.0 * np.pi * (k1 * lag[None, :] % LENGTH) / LENGTH
    b = 2.0 * np.pi * (lag[:, None] * l % LANES) / LANES
    table["gain_left"] = np.stack(
        [np.concatenate([np.cos(a), -np.sin(a)], axis=1), np.concatenate([np.sin(a), np.cos(a)], axis=1)]
    )
    table["gain_right"] = np.concatenate([np.cos(b), np.sin(b)], axis=0)
    p = np.arange(nproj)
    gap = (p[:, None] - p[None, :]) % nproj
    near = (np.minimum(gap, nproj - gap) <= ANGLE_TAPS // 2).astype(np.float32).astype(jnp.bfloat16)
    table["box"] = np.concatenate([near, near], axis=1)
    return {k: v.astype(np.float32) if v.dtype == np.float64 else v for k, v in table.items()}


def vmem_spec():
    return pl.BlockSpec(memory_space=pltpu.VMEM)


def smem_spec():
    return pl.BlockSpec(memory_space=pltpu.SMEM)


def local(projections, correlation, offset, smooth_taps):
    ang, row = lax.axis_size("ang"), lax.axis_size("row")
    here = lax.axis_index("row")
    per, rows, width = projections.shape
    nproj = per * ang
    seam_cols = LEFT * LANES

    halo = jnp.where(here == 0, projections[:, rows - REACH :], projections[:, :REACH])
    half_turn = [(i, (i + ang // 2) % ang) for i in range(ang)]
    across = [(i, 1 - i) for i in range(row)]
    both = [(a * row + r, b * row + s) for a, b in half_turn for r, s in across]
    seam_halo = lax.ppermute(halo[:, :, :seam_cols], ("ang", "row"), both)
    seam = lax.ppermute(projections[:, :, :seam_cols], "ang", half_turn)
    halo = lax.ppermute(halo, "row", across)

    taps = smooth_taps / jnp.sum(smooth_taps, axis=1, keepdims=True)
    ints = jnp.concatenate([correlation, offset, here[None].astype(jnp.int32)])
    sent = pl.pallas_call(
        source_kernel,
        out_shape=jax.ShapeDtypeStruct((rows * per * BLOCKS, LANES), f32),
        in_specs=[smem_spec(), smem_spec()] + [vmem_spec()] * 4,
        out_specs=vmem_spec(),
        compiler_params=pltpu.CompilerParams(vmem_limit_bytes=40 * 1024 * 1024),
        name="source",
    )(ints, taps, projections, halo, seam, seam_halo)

    got = lax.all_to_all(sent.reshape(rows, per * BLOCKS, LANES), "ang", split_axis=0, concat_axis=0, tiled=True)
    got = got.reshape(nproj * BLOCKS, LANES)

    t = tables(nproj)
    left = (t["gain_left"] * jnp.tile(taps[0], 2)).reshape(2 * OUTER, 2 * TAPS)
    gain = jnp.dot(left, t["gain_right"], precision=lax.Precision.HIGHEST) * jnp.tile(t["ramp"], (2, 1))
    ends = jnp.zeros(t["tap_at"].shape, f32)
    for k in range(TAPS):
        ends = jnp.where(t["tap_at"] == k, taps[0, k], ends)

    out = pl.pallas_call(
        sinogram_kernel,
        out_shape=jax.ShapeDtypeStruct((nproj, LENGTH), f32),
        in_specs=[vmem_spec()] * 13,
        out_specs=vmem_spec(),
        scratch_shapes=[
            pltpu.VMEM((OUTER, nproj, LANES), f32),
            pltpu.VMEM((OUTER, 8, LANES), f32),
            pltpu.VMEM((OUTER, 8, LANES), f32),
            pltpu.VMEM((OUTER, 8, 2 * LANES), f32),
            pltpu.VMEM((nproj // 2, 2 * LANES), f32),
        ],
        compiler_params=pltpu.CompilerParams(vmem_limit_bytes=56 * 1024 * 1024),
        name="sinogram",
    )(
        got, gain[:OUTER], gain[OUTER:], t["ramp"], ends, t["twist_re"], t["twist_im"], t["end_u"], t["end_v"],
        t["box"], t["forward"], t["backward"], t["end_w"],
    )
    return out[None, None]


def solution(mesh):
    P = jax.sharding.PartitionSpec
    placed = (P("ang", "row", None), P("ang"), P("ang"), P())
    return jax.shard_map(
        local, mesh=mesh, in_specs=placed, out_specs=P("row", "ang", None, None), check_vma=False
    )
```

profile of v0, /device:TPU:1, one launch (start us, length us, event | category | flops | bytes accessed | tf_op | source)
XLA Modules:
  0.0 100.7 jit_solution(14883127322278675879)
XLA Ops:
  0.0 0.0 copy-start
  0.0 1.4 %slice_select_fusion = f32[2,16,4096]{2,1,0:T(8,128)S(1)} fusion(f32[2,64,4096]{2,1,0:T(8,128)} %own.1, pred[]{:T(512)S(6)} %eq.3), kind=kLoop, calls=%fused_computation.2 | loop fusion | flops 131072 | bytes 1572865 | tf_op jit(solution)/shard_map/jit(_where)/select_n | solution.py:345
  1.4 3.8 %collective-permute-start = (f32[2,16,4096]{2,1,0:T(8,128)S(1)}, f32[2,16,4096]{2,1,0:T(8,128)S(1)}, u32[]{:S(2)}, u32[]{:S(2)}) collective-permute-start(f32[2,16,4096]{2,1,0:T(8,128)S(1)} %slice_select_fusion), channel_id=1, source_target_pairs={{0,1},{1,0},{2,3},{3,2},{4,5},{5,4},{6,7},{7,6},{8,9},{9,8},{10,11... | collective-permute-start | bytes 1572872 | tf_op jit(solution)/shard_map/ppermute | solution.py:351
  5.2 1.7 %slice.122 = f32[2,64,512]{2,1,0:T(8,128)} slice(f32[2,64,4096]{2,1,0:T(8,128)} %own.1), slice={[0:2], [0:64], [0:512]} | slice | bytes 524288 | tf_op jit(solution)/shard_map/slice | solution.py:350
  6.9 0.4 collective-permute-start.1
  7.3 0.6 slice.160
  7.9 0.4 collective-permute-start.2
  8.3 0.8 reduce_sum.9
  9.1 0.7 broadcast_divide_fusion.taps
  9.9 0.8 pad_add_fusion.ints
  10.6 8.4 %collective-permute-done.2.seam_halo = f32[2,16,512]{2,1,0:T(8,128)S(1)} collective-permute-done((f32[2,16,512]{2,1,0:T(8,128)}, f32[2,16,512]{2,1,0:T(8,128)S(1)}, u32[]{:S(2)}, u32[]{:S(2)}) %collective-permute-start.2) | collective-permute-done | bytes 65568 | tf_op jit(solution)/shard_map/ppermute | solution.py:349
  19.0 3.6 %collective-permute-done.1.seam = f32[2,64,512]{2,1,0:T(8,128)S(1)} collective-permute-done((f32[2,64,512]{2,1,0:T(8,128)}, f32[2,64,512]{2,1,0:T(8,128)S(1)}, u32[]{:S(2)}, u32[]{:S(2)}) %collective-permute-start.1) | collective-permute-done | bytes 262176 | tf_op jit(solution)/shard_map/ppermute | solution.py:350
  22.6 0.0 collective-permute-done.halo
  22.6 0.0 copy-done
  22.6 11.1 %source.1 = f32[4608,128]{1,0:T(8,128)} custom-call(s32[5]{0:T(128)S(1)} %pad_add_fusion.ints, f32[2,33]{1,0:T(2,128)S(1)} %broadcast_divide_fusion.taps, f32[2,64,4096]{2,1,0:T(8,128)S(1)} %copy-done, f32[2,16,4096]{2,1,0:T(8,128)S(1)} %collective-permute-done.halo, f32[2,64,512]{2,1,0:T(8,128)S(1)} %collective-permute-done.1.seam, ...), custom_call_target="tpu_custom_call" | custom-call | tf_op jit(solution)/shard_map/source/pallas_call | solution.py:355
  33.7 0.0 copy-start.3
  33.7 0.0 copy-start.4
  33.7 0.0 copy-start.5
  33.7 0.0 copy-start.6
  33.7 0.0 copy-start.7
  33.7 0.0 copy-start.8
  33.7 0.0 copy-start.9
  33.7 0.0 copy-start.10
  33.7 0.0 copy-start.11
  33.8 10.8 %all-to-all-start = ((f32[64,72,128]{2,1,0:T(8,128)}), f32[64,72,128]{2,1,0:T(8,128)S(1)}, u32[]{:S(2)}, u32[]{:S(2)}) async-start(f32[64,72,128]{2,1,0:T(8,128)} %bitcast.1), calls=%async_computation | async-start | bytes 4718592 | tf_op jit(solution)/shard_map/all_to_all | solution.py:364
  44.6 0.1 mul.13
  44.7 0.7 fusion.2
  45.4 0.7 fusion.1
  46.1 0.0 copy-done.3
  46.1 0.0 copy-done.4
  46.1 0.0 copy-done.5
  46.1 0.0 copy-done.6
  46.1 0.0 copy-done.7
  46.1 0.0 copy-done.8
  46.2 0.0 copy-done.9
  46.2 0.0 copy-done.10
  46.2 0.0 copy-done.11
  46.2 0.0 copy-start.12
  46.2 0.0 copy-start.2
  46.2 0.0 copy-start.13
  46.2 24.3 %select_select_fusion.ends = f32[512,256]{1,0:T(8,128)} fusion(pred[512,256]{1,0:T(32,128)(4,1)S(1)} %copy-done.3, pred[512,256]{1,0:T(32,128)(4,1)S(1)} %copy-done.4, pred[512,256]{1,0:T(32,128)(4,1)S(1)} %copy-done.5, pred[512,256]{1,0:T(32,128)(4,1)S(1)} %copy-done.6, pred[512,256]{1,0:T(32,128)(4,1)S(1)} %copy-done.7, pred[512,256]{1,0:T(32,128)(4,1)S(1)} %copy-done.8, ...), kind=kLoop, calls=%fused_computation.1 | loop fusion | flops 4194304 | bytes 4718720 | tf_op jit(solution)/shard_map/jit(_where)/select_n | solution.py:372
  70.5 0.0 copy-done.12
  70.5 0.0 copy-done.2
  70.6 0.0 copy-done.13
  70.6 0.2 convolution_multiply_fusion
  70.8 0.6 fusion
  71.4 4.5 %all-to-all-done = f32[64,72,128]{2,1,0:T(8,128)S(1)} async-done(((f32[64,72,128]{2,1,0:T(8,128)}), f32[64,72,128]{2,1,0:T(8,128)S(1)}, u32[]{:S(2)}, u32[]{:S(2)}) %all-to-all-start) | async-done | bytes 2359328 | tf_op jit(solution)/shard_map/all_to_all | solution.py:364
  75.9 0.0 copy-start.1
  75.9 1.4 %copy-done.1 = f32[64,72,128]{2,1,0:T(8,128)} copy-done((f32[64,72,128]{2,1,0:T(8,128)}, f32[64,72,128]{2,1,0:T(8,128)S(1)}, u32[]{:S(2)}) %copy-start.1) | copy-done | bytes 2359320
  77.4 23.4 %sinogram.1 = f32[128,8192]{1,0:T(8,128)} custom-call(f32[4608,128]{1,0:T(8,128)} %bitcast.42, f32[64,128]{1,0:T(8,128)} %get-tuple-element.6.gain_re, f32[64,128]{1,0:T(8,128)} %get-tuple-element.5.gain_im, f32[64,128]{1,0:T(8,128)} %constant.99.clone.ramp, f32[512,256]{1,0:T(8,128)} %select_select_fusion.ends, f32[64,128]{1,0:T(8,128)} %constant.133.clone.twist_re, ...), custom_call_target="tpu_custom_call" | custom-call | tf_op jit(solution)/shard_map/sinogram/pallas_call | solution.py:374
  (4 shorter events, 0.0 us)
Async XLA Ops:
  0.0 22.6 %copy-start = (f32[2,64,4096]{2,1,0:T(8,128)S(1)}, f32[2,64,4096]{2,1,0:T(8,128)}, u32[]{:S(2)}) copy-start(f32[2,64,4096]{2,1,0:T(8,128)} %own.1) | copy-start | bytes 6291460
  1.4 21.2 %collective-permute-start = (f32[2,16,4096]{2,1,0:T(8,128)S(1)}, f32[2,16,4096]{2,1,0:T(8,128)S(1)}, u32[]{:S(2)}, u32[]{:S(2)}) collective-permute-start(f32[2,16,4096]{2,1,0:T(8,128)S(1)} %slice_select_fusion), channel_id=1, source_target_pairs={{0,1},{1,0},{2,3},{3,2},{4,5},{5,4},{6,7},{7,6},{8,9},{9,8},{10,11... | collective-permute-start | bytes 1572872 | tf_op jit(solution)/shard_map/ppermute | solution.py:351
  6.9 15.7 %collective-permute-start.1 = (f32[2,64,512]{2,1,0:T(8,128)}, f32[2,64,512]{2,1,0:T(8,128)S(1)}, u32[]{:S(2)}, u32[]{:S(2)}) collective-permute-start(f32[2,64,512]{2,1,0:T(8,128)} %slice.122), channel_id=1, source_target_pairs={{0,64},{2,66},{4,68},{6,70},{8,72},{10,74},{12,76},{14,78},{16,80}... | collective-permute-start | bytes 786440 | tf_op jit(solution)/shard_map/ppermute | solution.py:350
  7.9 11.1 %collective-permute-start.2 = (f32[2,16,512]{2,1,0:T(8,128)}, f32[2,16,512]{2,1,0:T(8,128)S(1)}, u32[]{:S(2)}, u32[]{:S(2)}) collective-permute-start(f32[2,16,512]{2,1,0:T(8,128)} %slice.160), channel_id=1, source_target_pairs={{0,65},{1,64},{2,67},{3,66},{4,69},{5,68},{6,71},{7,70},{8,73},{9,... | collective-permute-start | bytes 196616 | tf_op jit(solution)/shard_map/ppermute | solution.py:349
  33.7 12.4 %copy-start.3 = (pred[512,256]{1,0:T(32,128)(4,1)S(1)}, pred[512,256]{1,0:T(32,128)(4,1)}, u32[]{:S(2)}) copy-start(pred[512,256]{1,0:T(32,128)(4,1)} %constant.132.clone) | copy-start | bytes 393220
  33.7 12.4 %copy-start.4 = (pred[512,256]{1,0:T(32,128)(4,1)S(1)}, pred[512,256]{1,0:T(32,128)(4,1)}, u32[]{:S(2)}) copy-start(pred[512,256]{1,0:T(32,128)(4,1)} %constant.131.clone) | copy-start | bytes 393220
  33.7 12.4 %copy-start.5 = (pred[512,256]{1,0:T(32,128)(4,1)S(1)}, pred[512,256]{1,0:T(32,128)(4,1)}, u32[]{:S(2)}) copy-start(pred[512,256]{1,0:T(32,128)(4,1)} %constant.130.clone) | copy-start | bytes 393220
  33.7 12.4 %copy-start.6 = (pred[512,256]{1,0:T(32,128)(4,1)S(1)}, pred[512,256]{1,0:T(32,128)(4,1)}, u32[]{:S(2)}) copy-start(pred[512,256]{1,0:T(32,128)(4,1)} %constant.129.clone) | copy-start | bytes 393220
  33.7 12.4 %copy-start.7 = (pred[512,256]{1,0:T(32,128)(4,1)S(1)}, pred[512,256]{1,0:T(32,128)(4,1)}, u32[]{:S(2)}) copy-start(pred[512,256]{1,0:T(32,128)(4,1)} %constant.128.clone) | copy-start | bytes 393220
  33.7 12.4 %copy-start.8 = (pred[512,256]{1,0:T(32,128)(4,1)S(1)}, pred[512,256]{1,0:T(32,128)(4,1)}, u32[]{:S(2)}) copy-start(pred[512,256]{1,0:T(32,128)(4,1)} %constant.127.clone) | copy-start | bytes 393220
  33.7 12.4 %copy-start.9 = (pred[512,256]{1,0:T(32,128)(4,1)S(1)}, pred[512,256]{1,0:T(32,128)(4,1)}, u32[]{:S(2)}) copy-start(pred[512,256]{1,0:T(32,128)(4,1)} %constant.126.clone) | copy-start | bytes 393220
  33.7 12.4 %copy-start.10 = (pred[512,256]{1,0:T(32,128)(4,1)S(1)}, pred[512,256]{1,0:T(32,128)(4,1)}, u32[]{:S(2)}) copy-start(pred[512,256]{1,0:T(32,128)(4,1)} %constant.125.clone) | copy-start | bytes 393220
  33.7 12.4 %copy-start.11 = (pred[512,256]{1,0:T(32,128)(4,1)S(1)}, pred[512,256]{1,0:T(32,128)(4,1)}, u32[]{:S(2)}) copy-start(pred[512,256]{1,0:T(32,128)(4,1)} %constant.124.clone) | copy-start | bytes 393220
  33.8 42.2 %all-to-all-start = ((f32[64,72,128]{2,1,0:T(8,128)}), f32[64,72,128]{2,1,0:T(8,128)S(1)}, u32[]{:S(2)}, u32[]{:S(2)}) async-start(f32[64,72,128]{2,1,0:T(8,128)} %bitcast.1), calls=%async_computation | async-start | bytes 4718592 | tf_op jit(solution)/shard_map/all_to_all | solution.py:364
  46.2 24.3 %copy-start.12 = (f32[2,64,66]{2,1,0:T(8,128)S(1)}, f32[2,64,66]{2,1,0:T(8,128)}, u32[]{:S(2)}) copy-start(f32[2,64,66]{2,1,0:T(8,128)} %constant.46.clone) | copy-start | bytes 101380
  46.2 24.4 %copy-start.2 = (f32[64,128]{1,0:T(8,128)S(1)}, f32[64,128]{1,0:T(8,128)}, u32[]{:S(2)}) copy-start(f32[64,128]{1,0:T(8,128)} %constant.99.clone.ramp) | copy-start | bytes 98308
  46.2 24.4 %copy-start.13 = (f32[66,128]{1,0:T(8,128)S(1)}, f32[66,128]{1,0:T(8,128)}, u32[]{:S(2)}) copy-start(f32[66,128]{1,0:T(8,128)} %constant.98.clone) | copy-start | bytes 101380
  75.9 1.4 %copy-start.1 = (f32[64,72,128]{2,1,0:T(8,128)}, f32[64,72,128]{2,1,0:T(8,128)S(1)}, u32[]{:S(2)}) copy-start(f32[64,72,128]{2,1,0:T(8,128)S(1)} %all-to-all-done) | copy-start | bytes 7077892
where the time goes:
time: 101 us
  Pallas kernels  34.4 us (34%)
  other arithmetic  28 us (28%)
  waiting for transfers between devices  16.5 us (16%)
  starting transfers between devices  15.4 us (15%)
  local copies, waits for them, and re-layouts  5.94 us (6%)
    select_n x1, other arithmetic, local(): ends = jnp.where(t['tap_at'] == k, taps[0, k], ends)  24.3 us
    pallas_call x1, Pallas kernels, local(): pl.pallas_call(sinogram_kernel, out_shape=jax.ShapeDtypeStruct((nproj, LE...  23.4 us
    pallas_call x1, Pallas kernels, local(): pl.pallas_call(source_kernel, out_shape=jax.ShapeDtypeStruct((rows * per...  11.1 us
    all_to_all x1, starting transfers between devices, local(): lax.all_to_all(sent.reshape(rows, per * BLOCKS, LANES), 'ang', split_axis...  10.8 us
    ppermute x1, waiting for transfers between devices, local(): seam_halo = lax.ppermute(halo[:, :, :seam_cols], ('ang', 'row'), both)  8.41 us
    all_to_all x1, waiting for transfers between devices, local(): lax.all_to_all(sent.reshape(rows, per * BLOCKS, LANES), 'ang', split_axis...  4.51 us
    ppermute x1, starting transfers between devices, local(): halo = lax.ppermute(halo, 'row', across)  3.82 us
    ppermute x1, waiting for transfers between devices, local(): seam = lax.ppermute(projections[:, :, :seam_cols], 'ang', half_turn)  3.59 us
  transfers between devices with their start and end apart: 4, of which 3 were waited for; matrix products, arithmetic and copies ran while one was open for 31% of the time, Pallas kernels for 0%

commit v1 on v0

v1 whole, which is shorter than its diff:
```python
import functools
import math

import jax
import jax.numpy as jnp
import numpy as np
from jax import lax
from jax.experimental import pallas as pl
from jax.experimental.pallas import tpu as pltpu

ANGLE_TAPS = 31
LANES = 128
OUTER = 64
BLOCKS = 36
LEFT = 4
REACH = 16
TAPS = 2 * REACH + 1
LENGTH = OUTER * LANES
MIN_OVERLAP_OFFSET = 127
TOGETHER = 2
f32, bf16 = jnp.float32, jnp.bfloat16


def halves(x):
    high = x.astype(bf16)
    return high, (x - high.astype(f32)).astype(bf16)


def thirds(x):
    high = x.astype(bf16)
    rest = x - high.astype(f32)
    middle = rest.astype(bf16)
    return high, middle, (rest - middle.astype(f32)).astype(bf16)


def mxu(a, b):
    return jnp.dot(a, b, preferred_element_type=f32)


def row_matrices(taps, rows, sources, place_of):
    target = lax.broadcasted_iota(jnp.int32, (rows, 3 * sources), 0)
    at = lax.broadcasted_iota(jnp.int32, (rows, 3 * sources), 1)
    third = at // sources
    tap_at = place_of(at - third * sources) - target + REACH
    matrix = jnp.zeros((rows, 3 * sources), f32)
    for t in range(TAPS):
        matrix = jnp.where(tap_at == t, taps[1, t], matrix)
    high, mid, low = (part.astype(f32) for part in thirds(matrix))
    one = jnp.where(third == 1, mid, high).astype(bf16)
    two = jnp.where(third == 0, low, jnp.where(third == 1, mid, high)).astype(bf16)
    return one, two


def row_filter(matrices, field):
    high, mid, low = thirds(field)
    one = jnp.concatenate([high, high, mid], axis=0)
    two = jnp.concatenate([high, mid, low], axis=0)
    return mxu(matrices[0], one) + mxu(matrices[1], two)


def block_of(refs, s, block):
    last = refs[0].shape[2] // LANES - 1
    at = jnp.clip(block, 0, last) * LANES
    if not isinstance(at, int):
        at = pl.multiple_of(at, LANES)
    parts = [ref[s, :, pl.ds(at, LANES)] for ref in refs]
    return parts[0] if len(parts) == 1 else jnp.concatenate(parts, axis=0)


class Shifted:
    def __init__(self, ints, s, refs):
        self.overlap, self.lead = ints[s], ints[2 + s]
        self.shift = self.overlap - self.lead
        self.skip = self.shift // LANES
        turn = self.shift - self.skip * LANES
        self.back = lax.rem(LANES - turn, LANES)
        self.lane = lax.broadcasted_iota(jnp.int32, (1, LANES), 1)
        self.keep = self.lane < LANES - turn
        self.s, self.refs = s, refs

    def turned(self, block):
        return pltpu.roll(block_of(self.refs, self.s, block + self.skip), self.back, 1)

    def column(self, b):
        return LANES * b + self.shift + self.lane

    def plain_pair(self, b, width):
        parts = [self.turned(b + j) for j in range(3)]
        logs = []
        for j in range(2):
            value = jnp.where(self.keep, parts[j], parts[j + 1])
            logs.append(-jnp.log(jnp.where(self.column(b + j) < width, value, 1.0)))
        return jnp.concatenate(logs, axis=1)


def early_kernel(ints, taps, own, out):
    rows, width = own.shape[1], own.shape[2]
    matrices = row_matrices(taps, rows, rows, lambda at: at)
    for s in range(2):
        moved = Shifted(ints, s, [own])

        def pair(i, carry, s=s, moved=moved):
            at = pl.ds(pl.multiple_of((i - 1) * 2 * LANES, 2 * LANES), 2 * LANES)
            out[s, :, at] = row_filter(matrices, moved.plain_pair(2 * i, width))
            return carry

        lax.fori_loop(1, width // LANES // 2, pair, 0, unroll=3)


def source_kernel(ints, taps, early, own, halo, seam, seam_halo, out):
    rows, halo_rows, width = own.shape[1], halo.shape[1], halo.shape[2]
    every = rows + halo_rows
    row_group = ints[4]
    lane = lax.broadcasted_iota(jnp.int32, (1, LANES), 1)

    def across(at):
        return jnp.where((at >= rows) & (row_group > 0), at - every, at)

    matrices = row_matrices(taps, rows, every, across)
    halo_matrices = row_matrices(taps, rows, halo_rows, lambda at: across(at + rows))

    for s in range(2):

        def store(b, value, s=s):
            for g in range(rows // 8):
                at = pl.ds(8 * g * 2 * BLOCKS + s * BLOCKS + LEFT + b, 8, stride=2 * BLOCKS)
                out[at, :] = value[8 * g : 8 * g + 8]

        moved = Shifted(ints, s, [own, halo.at[:, :, : own.shape[2]]])
        overlap, lead, shift = moved.overlap, moved.lead, moved.shift
        mirror = jnp.broadcast_to((lead - 1 - lane) & (LANES - 1), (every, LANES))
        flipped = [
            jnp.take_along_axis(block_of([seam, seam_halo], s, j), mirror, axis=1, mode="promise_in_bounds")
            for j in range(LEFT)
        ]

        def blended(b, first, second):
            weight = jnp.clip((moved.column(b).astype(f32) + 0.5) / overlap.astype(f32), 0.0, 1.0)
            mine = jnp.where(moved.keep, first, second)
            other = jnp.where(lane < lead, flipped[min(max(-b, 0), 3)], flipped[min(max(-b - 1, 0), 3)])
            return -jnp.log(weight * mine + (1.0 - weight) * other)

        for b in range(-LEFT, 2, 2):
            parts = [moved.turned(b + i) for i in range(3)]
            logs = [blended(b + i, parts[i], parts[i + 1]) for i in range(2)]
            value = row_filter(matrices, jnp.concatenate(logs, axis=1))
            store(b, value[:, :LANES])
            store(b + 1, value[:, LANES:])

        rest = Shifted(ints, s, [halo])

        def pair(i, carry, s=s, store=store, rest=rest):
            b = 2 * i
            at = pl.ds(pl.multiple_of((b - 2) * LANES, 2 * LANES), 2 * LANES)
            value = early[s, :, at] + row_filter(halo_matrices, rest.plain_pair(b, width))
            store(b, value[:, :LANES])
            value = value[:, LANES:]
            last = b + 2 == width // LANES
            value = jnp.where(last & (lane == LANES - 1), rest.shift.astype(f32), value)
            value = jnp.where(last & (lane == LANES - 2) & (rest.shift > 1), rest.lead.astype(f32), value)
            store(b + 1, value)
            return carry

        lax.fori_loop(1, width // LANES // 2, pair, 0, unroll=15)


def times(a, b):
    return (a[0] * b[0] - a[1] * b[1], a[0] * b[1] + a[1] * b[0])


def dft(x, sign):
    n = len(x)
    if n == 1:
        return x
    even, odd = dft(x[0::2], sign), dft(x[1::2], sign)
    root = math.sqrt(0.5)
    first, second = [], []
    for k in range(n // 2):
        re, im = odd[k]
        if 4 * k == n:
            re, im = -sign * im, sign * re
        elif 8 * k == n:
            re, im = root * (re - sign * im), root * (im + sign * re)
        elif 8 * k == 3 * n:
            re, im = root * (-re - sign * im), root * (-im + sign * re)
        first.append((even[k][0] + re, even[k][1] + im))
        second.append((even[k][0] - re, even[k][1] - im))
    return first + second


def small_twist(value, power, sign):
    if power % OUTER == 0:
        return value
    angle = sign * 2.0 * math.pi * (power % OUTER) / OUTER
    return times(value, (np.float32(math.cos(angle)), np.float32(math.sin(angle))))


def sinogram_kernel(
    x, table, weights, out_hbm, out, field, mid_re, mid_im, rows, end_rows, sent
):
    gain_re, gain_im, twist_re, twist_im, end_u, end_v, ramp, _ = (
        table.at[OUTER * (k // 2) : OUTER * (k // 2 + 1), LANES * (k % 2) : LANES * (k % 2 + 1)] for k in range(8)
    )
    box = weights.at[: 2 * OUTER]
    forward, backward = ([weights.at[(at + k) * 2 * LANES - LANES : (at + k + 1) * 2 * LANES - LANES] for k in range(2)] for at in (1, 3))
    end_w = weights.at[5 * 2 * LANES - LANES :]
    half = out.shape[0] // 2
    lane = lax.broadcasted_iota(jnp.int32, (8, LANES), 1)

    def place(g, carry):
        sides = []
        for side in range(2):
            start = (side * half + 8 * g) * BLOCKS
            blocks = [x[pl.ds(start + k, 8, stride=BLOCKS), :] for k in range(BLOCKS)]
            last = blocks[-1]
            shift = last[:, LANES - 1 :]
            lead = jnp.where(shift > 1.5, last[:, LANES - 2 : LANES - 1], float(MIN_OVERLAP_OFFSET))
            hidden = (lane == LANES - 1) | ((lane == LANES - 2) & (shift > 1.5))
            blocks[-1] = jnp.where(hidden, 0.0, last)
            sides.append((blocks, shift.astype(jnp.int32), lead.astype(jnp.int32)))
        for side in range(2):
            mine, _, lead = sides[side]
            theirs, their_shift, _ = sides[1 - side]
            at = pl.ds(pl.multiple_of(side * half + 8 * g, 8), 8)
            spot = LANES - 1 + lead - their_shift - lane
            index = spot & (LANES - 1)
            jump = (spot >> 7) + 4
            mirrored = {}
            for k in range(OUTER // 2):
                mirrored[k] = jnp.take_along_axis(theirs[LEFT + k], index, axis=1, mode="promise_in_bounds")
            mirrored[-1] = mirrored[0]
            mirrored[OUTER // 2] = jnp.zeros((8, LANES), f32)
            for step in (1, 2, 4):
                moved = (jump & step) != 0
                top = OUTER // 2
                mirrored = {
                    k: jnp.where(moved, mirrored[min(k + step, top)], mirrored[k]) for k in mirrored
                }
            for c in range(OUTER // 2 - LEFT + 1):
                value = mirrored[OUTER // 2 - 5 - c]
                if c == OUTER // 2 - LEFT:
                    value = jnp.where(lane >= lead, mine[0], value)
                field[c, at, :] = value
            for k in range(1, BLOCKS):
                field[OUTER // 2 - LEFT + k, at, :] = mine[k]
        return carry

    lax.fori_loop(0, half // 8, place, 0)

    def highpass(i, carry):
        both = jnp.concatenate([field[2 * i], field[2 * i + 1]], axis=1)
        high, low = halves(both)
        sums = mxu(box[...], jnp.concatenate([high, low], axis=0))
        both = both - sums * np.float32(1.0 / ANGLE_TAPS)
        field[2 * i] = both[:, :LANES]
        field[2 * i + 1] = both[:, LANES:]
        return carry

    lax.fori_loop(0, OUTER // 2, highpass, 0, unroll=8)

    edge = lax.broadcasted_iota(jnp.int32, (1, LANES), 1) < LANES // 2
    border = [jnp.where(edge, field[0, at : at + half], field[OUTER - 1, at : at + half]) for at in (0, half)]
    tail_of = [table[4 * OUTER :, LANES * k : LANES * (k + 1)] for k in range(2)]
    tails = jnp.dot(border[0], tail_of[0], precision=lax.Precision.HIGHEST, preferred_element_type=f32)
    tails += jnp.dot(border[1], tail_of[1], precision=lax.Precision.HIGHEST, preferred_element_type=f32)
    end_rows[:, :LANES] = tails
    end_rows[:, LANES:] = pltpu.roll(tails, 2 * REACH, 1)

    def outer_forward(low_at, high_at, mid_re, mid_im, rows):
        for b in range(8):
            got = dft([(field[8 * a + b, low_at, :], field[8 * a + b, high_at, :]) for a in range(8)], -1.0)
            for d in range(8):
                mid_re[8 * d + b], mid_im[8 * d + b] = small_twist(got[d], d * b, -1.0)
        for d in range(8):
            got = dft([(mid_re[8 * d + b], mid_im[8 * d + b]) for b in range(8)], -1.0)
            for e in range(8):
                k = d + 8 * e
                re, im = times(got[e], (twist_re[k : k + 1, :], twist_im[k : k + 1, :]))
                rows[k, :, :LANES] = re
                rows[k, :, LANES:] = im

    def inner(low_at, rows):
        for part in range(2):
            n = OUTER // 2
            span = slice(part * n, (part + 1) * n)
            high, low = halves(rows[span].reshape(n * 8, 2 * LANES))
            spectrum = mxu(high, forward[0][...]) + mxu(low, forward[0][...]) + mxu(high, forward[1][...])
            spectrum = spectrum.reshape(n, 8, 2 * LANES)
            here = end_rows[low_at, :]
            tail = here[None, :, :LANES] * end_u[span][:, None, :] + here[None, :, LANES:] * end_v[span][:, None, :]
            tail = tail.reshape(n * 8, LANES)
            t_high = tail.astype(bf16).astype(f32)
            front = lax.broadcasted_iota(jnp.int32, (1, LANES), 1) < LANES // 2
            t_one = jnp.where(front, t_high, tail - t_high).astype(bf16)
            t_two = jnp.where(front, t_high, 0.0).astype(bf16)
            wrapped = mxu(jnp.concatenate([t_one, t_two], axis=1), end_w[...]).reshape(n, 8, 2 * LANES)
            g_re, g_im, r = gain_re[span][:, None, :], gain_im[span][:, None, :], ramp[span][:, None, :]
            re, im = times((spectrum[..., :LANES], spectrum[..., LANES:]), (g_re, g_im))
            re = re - r * wrapped[..., :LANES]
            im = im - r * wrapped[..., LANES:]
            high, low = halves(jnp.concatenate([re, im], axis=2).reshape(n * 8, 2 * LANES))
            signal = mxu(high, backward[0][...]) + mxu(low, backward[0][...]) + mxu(high, backward[1][...])
            signal = signal.reshape(n, 8, 2 * LANES)
            re, im = times(
                (signal[..., :LANES], signal[..., LANES:]), (twist_re[span][:, None, :], -twist_im[span][:, None, :])
            )
            rows[span, :, :LANES] = re
            rows[span, :, LANES:] = im

    def outer_backward(low_at, high_at, mid_re, mid_im, rows):
        for d in range(8):
            got = dft([(rows[d + 8 * e, :, :LANES], rows[d + 8 * e, :, LANES:]) for e in range(8)], 1.0)
            for b in range(8):
                mid_re[8 * d + b], mid_im[8 * d + b] = small_twist(got[b], d * b, 1.0)
        for b in range(8):
            got = dft([(mid_re[8 * d + b], mid_im[8 * d + b]) for d in range(8)], 1.0)
            for a in range(8):
                c = 8 * a + b
                out[low_at, c * LANES : (c + 1) * LANES] = got[a][0]
                out[high_at, c * LANES : (c + 1) * LANES] = got[a][1]

    def copies(g):
        for side in range(2):
            at = pl.ds(pl.multiple_of(side * half + 8 * g, 8), 8)
            yield pltpu.make_async_copy(out.at[at], out_hbm.at[at], sent.at[side, g])

    def filtered(i, carry):
        spots = []
        for j in range(TOGETHER):
            g = TOGETHER * i + j
            low_at = pl.ds(pl.multiple_of(8 * g, 8), 8)
            high_at = pl.ds(pl.multiple_of(half + 8 * g, 8), 8)
            spots.append((low_at, high_at, mid_re.at[j], mid_im.at[j], rows.at[j]))
        for spot in spots:
            outer_forward(*spot)
        for spot in spots:
            inner(spot[0], spot[4])
        for spot in spots:
            outer_backward(*spot)
        for j in range(TOGETHER):
            for copy in copies(TOGETHER * i + j):
                copy.start()
        return carry

    lax.fori_loop(0, half // 8 // TOGETHER, filtered, 0)
    for g in range(half // 8):
        for copy in copies(g):
            copy.wait()


@functools.lru_cache(maxsize=None)
def tables(nproj):
    k1 = np.arange(OUTER)[:, None]
    l = np.arange(LANES)[None, :]
    angle = 2.0 * np.pi * (k1 * l % LENGTH) / LENGTH
    table = dict(twist_re=np.cos(angle), twist_im=-np.sin(angle))
    inner = 2.0 * np.pi * (np.arange(LANES)[:, None] * l % LANES) / LANES
    cos, sin = np.cos(inner), np.sin(inner)
    forward = np.block([[cos, -sin], [sin, cos]])
    backward = np.block([[cos, sin], [-sin, cos]])

    def two(w):
        high = w.astype(np.float32).astype(jnp.bfloat16)
        low = (w - high.astype(np.float64)).astype(np.float32).astype(jnp.bfloat16)
        return high, low

    table["forward"] = np.stack(two(forward))
    table["backward"] = np.stack(two(backward))
    columns = np.concatenate([np.arange(REACH), LENGTH - REACH + np.arange(REACH)])
    some = columns % LANES
    end_w = np.concatenate([forward[some], forward[LANES + some]], axis=0)
    high, low = two(end_w)
    table["end_w"] = np.concatenate([high, high, low, np.zeros_like(low)], axis=0)
    theta = 2.0 * np.pi * (k1 * columns[None, :] % LENGTH) / LENGTH
    table["end_u"] = np.tile(np.cos(theta), (1, 4))
    table["end_v"] = np.tile(np.concatenate([np.sin(theta), -np.sin(theta)], axis=1), (1, 2))
    tap_at = np.full((LANES, 2, 4, 2 * REACH), -1, np.int32)
    for i in range(REACH):
        for group in range(4):
            for t in range(TAPS):
                if LANES - REACH + i + t < LANES:
                    tap_at[LANES - REACH + i + t, group % 2, group, i] = t
                if i + t - 2 * REACH >= 0:
                    tap_at[i + t - 2 * REACH, group % 2, group, REACH + i] = t
    table["tap_at"] = tap_at.reshape(LANES, 2 * LANES)
    frequency = k1 + OUTER * l
    table["ramp"] = np.minimum(frequency, LENGTH - frequency) / (LENGTH / 2) / LENGTH
    lag = np.arange(TAPS) - REACH
    a = 2.0 * np.pi * (k1 * lag[None, :] % LENGTH) / LENGTH
    b = 2.0 * np.pi * (lag[:, None] * l % LANES) / LANES
    table["gain_left"] = np.stack(
        [np.concatenate([np.cos(a), -np.sin(a)], axis=1), np.concatenate([np.sin(a), np.cos(a)], axis=1)]
    )
    table["gain_right"] = np.concatenate([np.cos(b), np.sin(b)], axis=0)
    p = np.arange(nproj)
    gap = (p[:, None] - p[None, :]) % nproj
    near = (np.minimum(gap, nproj - gap) <= ANGLE_TAPS // 2).astype(np.float32).astype(jnp.bfloat16)
    table["box"] = np.concatenate([near, near], axis=1)
    pairs = (("twist_re", "twist_im"), ("end_u", "end_v"), ("ramp", "ramp"))
    fixed = np.block([[table[k] for k in pair] for pair in pairs]).astype(np.float32)
    weights = np.concatenate([table["box"], *table["forward"], *table["backward"], table["end_w"]], axis=0)
    gain = [table[k].astype(np.float32) for k in ("gain_left", "gain_right")]
    return fixed, weights, gain, table["tap_at"]


def vmem_spec():
    return pl.BlockSpec(memory_space=pltpu.VMEM)


def hbm_spec():
    return pl.BlockSpec(memory_space=pltpu.MemorySpace.HBM)


def smem_spec():
    return pl.BlockSpec(memory_space=pltpu.SMEM)


def early_side(ints, taps, projections):
    per, rows, width = projections.shape
    shape = jax.ShapeDtypeStruct((per, rows, width - 2 * LANES), f32)
    return pl.pallas_call(
        early_kernel,
        out_shape=shape,
        in_specs=[smem_spec(), smem_spec(), vmem_spec()],
        out_specs=vmem_spec(),
        compiler_params=pltpu.CompilerParams(vmem_limit_bytes=24 * 1024 * 1024),
        cost_estimate=pl.CostEstimate(flops=12 * per * rows * rows * width, bytes_accessed=8 * per * rows * width, transcendentals=per * rows * width),
        name="early",
    )(ints, taps, projections)


def source_side(ints, taps, early, projections, halo, seam, seam_halo):
    per, rows, _ = projections.shape
    return pl.pallas_call(
        source_kernel,
        grid=(1,),
        out_shape=jax.ShapeDtypeStruct((rows * per * BLOCKS, LANES), f32),
        in_specs=[smem_spec(), smem_spec(), vmem_spec(), pl.BlockSpec((per, rows, 8 * LANES), lambda i: (0, 0, 0))]
        + [vmem_spec()] * 3,
        out_specs=vmem_spec(),
        compiler_params=pltpu.CompilerParams(vmem_limit_bytes=24 * 1024 * 1024),
        name="source",
    )(ints, taps, early, projections, halo, seam, seam_halo)


def sinogram_side(got, taps):
    nproj = got.shape[0] // BLOCKS
    fixed, weights, (gain_left, gain_right), tap_at = tables(nproj)
    left = (gain_left * jnp.tile(taps[0], 2)).reshape(2 * OUTER, 2 * TAPS)
    gain = jnp.dot(left, gain_right, precision=lax.Precision.HIGHEST) * jnp.tile(fixed[2 * OUTER :, :LANES], (2, 1))
    ends = jnp.zeros(tap_at.shape, f32)
    for k in range(TAPS):
        ends = jnp.where(tap_at == k, taps[0, k], ends)
    table = jnp.concatenate([jnp.concatenate([gain[:OUTER], gain[OUTER:]], axis=1), fixed, ends], axis=0)
    return pl.pallas_call(
        sinogram_kernel,
        out_shape=jax.ShapeDtypeStruct((nproj, LENGTH), f32),
        in_specs=[vmem_spec()] * 3,
        out_specs=hbm_spec(),
        scratch_shapes=[
            pltpu.VMEM((nproj, LENGTH), f32),
            pltpu.VMEM((OUTER, nproj, LANES), f32),
            pltpu.VMEM((TOGETHER, OUTER, 8, LANES), f32),
            pltpu.VMEM((TOGETHER, OUTER, 8, LANES), f32),
            pltpu.VMEM((TOGETHER, OUTER, 8, 2 * LANES), f32),
            pltpu.VMEM((nproj // 2, 2 * LANES), f32),
            pltpu.SemaphoreType.DMA((2, nproj // 16)),
        ],
        compiler_params=pltpu.CompilerParams(vmem_limit_bytes=28 * 1024 * 1024),
        name="sinogram",
    )(got, table, jnp.asarray(weights))


def local(projections, correlation, offset, smooth_taps):
    ang, row = lax.axis_size("ang"), lax.axis_size("row")
    here = lax.axis_index("row")
    per, rows, width = projections.shape
    nproj = per * ang
    seam_cols = LEFT * LANES

    halo = jnp.where(here == 0, projections[:, rows - REACH :], projections[:, :REACH])
    half_turn = [(i, (i + ang // 2) % ang) for i in range(ang)]
    across = [(i, 1 - i) for i in range(row)]
    both = [(a * row + r, b * row + s) for a, b in half_turn for r, s in across]
    seam_halo = lax.ppermute(halo[:, :, :seam_cols], ("ang", "row"), both)
    seam = lax.ppermute(projections[:, :, :seam_cols], "ang", half_turn)
    halo = lax.ppermute(halo, "row", across)

    taps = smooth_taps / jnp.sum(smooth_taps, axis=1, keepdims=True)
    ints = jnp.concatenate([correlation, offset, here[None].astype(jnp.int32)])
    early = early_side(ints, taps, projections)
    sent = source_side(ints, taps, early, projections, halo, seam, seam_halo)
    got = lax.all_to_all(sent.reshape(rows, per * BLOCKS, LANES), "ang", split_axis=0, concat_axis=0, tiled=True)
    return sinogram_side(got.reshape(nproj * BLOCKS, LANES), taps)[None, None]


def solution(mesh):
    P = jax.sharding.PartitionSpec
    placed = (P("ang", "row", None), P("ang"), P("ang"), P())
    return jax.shard_map(
        local, mesh=mesh, in_specs=placed, out_specs=P("row", "ang", None, None), check_vma=False
    )
```

time: 101 us -> 84 us (0.83)
  Pallas kernels: 34.4 us -> 21.3 us
  other arithmetic: 28 us -> 26.1 us
  local copies, waits for them, and re-layouts: 5.94 us -> 4.67 us
  waiting for transfers between devices: 16.5 us -> 15.3 us
    pallas_call x2 -> x3, Pallas kernels: 34.4 us -> 21.3 us  [the longest x1 15 us: sinogram_side(): pl.pallas_call(sinogram_kernel, out_shape=jax.ShapeDtypeStruct((nproj, LE...]
    ppermute x1, waiting for transfers between devices: 8.41 us -> 4.62 us  [local(): seam_halo = lax.ppermute(halo[:, :, :seam_cols], ('ang', 'row'), both)]
    select_n x1, other arithmetic: 24.3 us -> 21.4 us  [sinogram_side(): ends = jnp.where(tap_at == k, taps[0, k], ends)]
    all_to_all x1, waiting for transfers between devices: 4.51 us -> 7.09 us  [local(): lax.all_to_all(sent.reshape(rows, per * BLOCKS, LANES), 'ang', split_axis...]
  transfers between devices with their start and end apart: 4 -> 4, of which waited for: 3 -> 3; matrix products, arithmetic and copies ran while one was open for 31% -> 34% of each run, Pallas kernels for 0% -> 5%
where the time goes in v1:
time: 84 us; the launch traced here: 83.3 us
  other arithmetic  26.1 us (31%)
  Pallas kernels  21.3 us (25%)
  starting transfers between devices  15.5 us (18%)
  waiting for transfers between devices  15.3 us (18%)
  local copies, waits for them, and re-layouts  4.67 us (6%)
    select_n x1, other arithmetic, sinogram_side(): ends = jnp.where(tap_at == k, taps[0, k], ends)  21.4 us
    pallas_call x1, Pallas kernels, sinogram_side(): pl.pallas_call(sinogram_kernel, out_shape=jax.ShapeDtypeStruct((nproj, LE...  15 us
    all_to_all x1, starting transfers between devices, local(): lax.all_to_all(sent.reshape(rows, per * BLOCKS, LANES), 'ang', split_axis...  10.8 us
    all_to_all x1, waiting for transfers between devices, local(): lax.all_to_all(sent.reshape(rows, per * BLOCKS, LANES), 'ang', split_axis...  7.09 us
    ppermute x1, waiting for transfers between devices, local(): seam_halo = lax.ppermute(halo[:, :, :seam_cols], ('ang', 'row'), both)  4.62 us
    pallas_call x1, Pallas kernels, early_side(): pl.pallas_call(early_kernel, out_shape=shape, in_specs=[smem_spec(), smem...  4.32 us
    ppermute x1, starting transfers between devices, local(): halo = lax.ppermute(halo, 'row', across)  3.82 us
    ppermute x1, waiting for transfers between devices, local(): seam = lax.ppermute(projections[:, :, :seam_cols], 'ang', half_turn)  3.59 us
  transfers between devices with their start and end apart: 4, of which 3 were waited for; matrix products, arithmetic and copies ran while one was open for 34% of the time, Pallas kernels for 5%

profile of v1, /device:TPU:1, one launch (start us, length us, event | category | flops | bytes accessed | tf_op | source)
XLA Modules:
  0.0 83.3 jit_solution(16792867306878010326)
XLA Ops:
  0.0 0.0 copy-start
  0.0 1.4 %slice_select_fusion = f32[2,16,4096]{2,1,0:T(8,128)S(1)} fusion(f32[2,64,4096]{2,1,0:T(8,128)} %own.3, pred[]{:T(512)S(6)} %eq.3), kind=kLoop, calls=%fused_computation.1 | loop fusion | flops 131072 | bytes 1572865 | tf_op jit(solution)/shard_map/jit(_where)/select_n | solution.py:481
  1.4 3.8 %collective-permute-start = (f32[2,16,4096]{2,1,0:T(8,128)S(1)}, f32[2,16,4096]{2,1,0:T(8,128)S(1)}, u32[]{:S(2)}, u32[]{:S(2)}) collective-permute-start(f32[2,16,4096]{2,1,0:T(8,128)S(1)} %slice_select_fusion), channel_id=1, source_target_pairs={{0,1},{1,0},{2,3},{3,2},{4,5},{5,4},{6,7},{7,6},{8,9},{9,8},{10,11... | collective-permute-start | bytes 1572872 | tf_op jit(solution)/shard_map/ppermute | solution.py:487
  5.2 1.7 %slice.122 = f32[2,64,512]{2,1,0:T(8,128)} slice(f32[2,64,4096]{2,1,0:T(8,128)} %own.3), slice={[0:2], [0:64], [0:512]} | slice | bytes 524288 | tf_op jit(solution)/shard_map/slice | solution.py:486
  6.9 0.4 collective-permute-start.1
  7.3 0.5 collective-permute-start.2
  7.8 0.8 reduce_sum.9
  8.6 0.7 broadcast_divide_fusion.taps
  9.3 0.8 pad_add_fusion.ints
  10.1 0.0 copy-done
  10.1 4.3 %early.1 = f32[2,64,3840]{2,1,0:T(8,128)S(1)} custom-call(s32[5]{0:T(128)S(1)} %pad_add_fusion.ints, f32[2,33]{1,0:T(2,128)S(1)} %broadcast_divide_fusion.taps, f32[2,64,4096]{2,1,0:T(8,128)S(1)} %copy-done), custom_call_target="tpu_custom_call" | custom-call | flops 402653184 | bytes 4194304 | tf_op jit(solution)/shard_map/early/pallas_call | solution.py:421
  14.4 4.6 %collective-permute-done.2.seam_halo = f32[2,16,512]{2,1,0:T(8,128)S(1)} collective-permute-done((f32[2,16,512]{2,1,0:T(8,128)S(1)}, f32[2,16,512]{2,1,0:T(8,128)S(1)}, u32[]{:S(2)}, u32[]{:S(2)}) %collective-permute-start.2) | collective-permute-done | bytes 65568 | tf_op jit(solution)/shard_map/ppermute | solution.py:485
  19.0 3.6 %collective-permute-done.1.seam = f32[2,64,512]{2,1,0:T(8,128)S(1)} collective-permute-done((f32[2,64,512]{2,1,0:T(8,128)}, f32[2,64,512]{2,1,0:T(8,128)S(1)}, u32[]{:S(2)}, u32[]{:S(2)}) %collective-permute-start.1) | collective-permute-done | bytes 262176 | tf_op jit(solution)/shard_map/ppermute | solution.py:486
  22.6 0.0 collective-permute-done.halo
  22.6 2.0 %source.1 = f32[4608,128]{1,0:T(8,128)S(1)} custom-call(s32[5]{0:T(128)S(1)} %pad_add_fusion.ints, f32[2,33]{1,0:T(2,128)S(1)} %broadcast_divide_fusion.taps, f32[2,64,3840]{2,1,0:T(8,128)S(1)} %early.1, f32[2,64,4096]{2,1,0:T(8,128)S(1)} %copy-done, f32[2,16,4096]{2,1,0:T(8,128)S(1)} %collective-permute-done.halo, ...), custom_call_target="tpu_custom_call" | custom-call | tf_op jit(solution)/shard_map/source/pallas_call | solution.py:434
  24.6 0.0 copy-start.1
  24.6 1.4 %copy-done.1 = f32[4608,128]{1,0:T(8,128)} copy-done((f32[4608,128]{1,0:T(8,128)}, f32[4608,128]{1,0:T(8,128)S(1)}, u32[]{:S(2)}) %copy-start.1) | copy-done | bytes 2359320
  26.0 0.0 copy-start.6
  26.0 0.0 copy-start.7
  26.0 0.0 copy-start.8
  26.0 0.0 copy-start.9
  26.0 0.0 copy-start.10
  26.1 0.0 copy-start.11
  26.1 0.0 copy-start.12
  26.1 0.0 copy-start.13
  26.1 0.0 copy-start.14
  26.1 0.0 copy-start.3
  26.1 0.0 copy-start.5
  26.1 0.0 copy-start.4
  26.1 10.8 %all-to-all-start = ((f32[64,72,128]{2,1,0:T(8,128)}), f32[64,72,128]{2,1,0:T(8,128)S(1)}, u32[]{:S(2)}, u32[]{:S(2)}) async-start(f32[64,72,128]{2,1,0:T(8,128)} %bitcast.43), calls=%async_computation | async-start | bytes 4718592 | tf_op jit(solution)/shard_map/all_to_all | solution.py:493
  37.0 0.0 copy-start.2
  37.0 0.1 mul.13
  37.1 0.7 fusion.2
  37.8 0.7 fusion.1
  38.5 0.0 copy-done.6
  38.5 0.0 copy-done.7
  38.5 0.0 copy-done.8
  38.5 0.0 copy-done.9
  38.5 0.0 copy-done.10
  38.5 0.0 copy-done.11
  38.6 0.0 copy-done.12
  38.6 0.0 copy-done.13
  38.6 0.0 copy-done.14
  38.6 21.4 %select_select_fusion = f32[128,256]{1,0:T(8,128)S(1)} fusion(pred[128,256]{1,0:T(32,128)(4,1)S(1)} %copy-done.6, pred[128,256]{1,0:T(32,128)(4,1)S(1)} %copy-done.7, pred[128,256]{1,0:T(32,128)(4,1)S(1)} %copy-done.8, pred[128,256]{1,0:T(32,128)(4,1)S(1)} %copy-done.9, pred[128,256]{1,0:T(32,128)(4,1)S(1)} %copy-done.10, ...), kind=kLoop, calls=%fused_computation.3 | loop fusion | flops 1048576 | bytes 1179776 | tf_op jit(solution)/shard_map/jit(_where)/select_n | solution.py:453
  60.0 0.0 copy-done.3
  60.0 0.0 copy-done.5
  60.0 0.0 copy-done.4
  60.1 0.2 convolution_multiply_fusion
  60.3 1.0 %pad_maximum_fusion.table = f32[384,256]{1,0:T(8,128)S(1)} fusion(f32[128,256]{1,0:T(8,128)S(1)} %select_select_fusion, f32[192,256]{1,0:T(8,128)} %constant.121.clone, f32[64,128]{1,0:T(8,128)S(1)} %get-tuple-element.6, f32[64,128]{1,0:T(8,128)S(1)} %get-tuple-element.5), kind=kLoop, calls=%fused_computation.2 | loop fusion | flops 294912 | bytes 786432 | tf_op jit(solution)/shard_map/concatenate | solution.py:454
  61.2 7.1 %all-to-all-done = f32[64,72,128]{2,1,0:T(8,128)S(1)} async-done(((f32[64,72,128]{2,1,0:T(8,128)}), f32[64,72,128]{2,1,0:T(8,128)S(1)}, u32[]{:S(2)}, u32[]{:S(2)}) %all-to-all-start) | async-done | bytes 2359328 | tf_op jit(solution)/shard_map/all_to_all | solution.py:493
  68.3 0.0 copy-done.2
  68.3 15.0 %sinogram.1 = f32[128,8192]{1,0:T(8,128)} custom-call(f32[4608,128]{1,0:T(8,128)S(1)} %bitcast.42, f32[384,256]{1,0:T(8,128)S(1)} %pad_maximum_fusion.table, bf16[1408,256]{1,0:T(8,128)(2,1)S(1)} %copy-done.2), custom_call_target="tpu_custom_call" | custom-call | tf_op jit(solution)/shard_map/sinogram/pallas_call | solution.py:455
  (6 shorter events, 0.0 us)
Async XLA Ops:
  0.0 10.1 %copy-start = (f32[2,64,4096]{2,1,0:T(8,128)S(1)}, f32[2,64,4096]{2,1,0:T(8,128)}, u32[]{:S(2)}) copy-start(f32[2,64,4096]{2,1,0:T(8,128)} %own.3) | copy-start | bytes 6291460
  1.4 21.2 %collective-permute-start = (f32[2,16,4096]{2,1,0:T(8,128)S(1)}, f32[2,16,4096]{2,1,0:T(8,128)S(1)}, u32[]{:S(2)}, u32[]{:S(2)}) collective-permute-start(f32[2,16,4096]{2,1,0:T(8,128)S(1)} %slice_select_fusion), channel_id=1, source_target_pairs={{0,1},{1,0},{2,3},{3,2},{4,5},{5,4},{6,7},{7,6},{8,9},{9,8},{10,11... | collective-permute-start | bytes 1572872 | tf_op jit(solution)/shard_map/ppermute | solution.py:487
  6.9 15.7 %collective-permute-start.1 = (f32[2,64,512]{2,1,0:T(8,128)}, f32[2,64,512]{2,1,0:T(8,128)S(1)}, u32[]{:S(2)}, u32[]{:S(2)}) collective-permute-start(f32[2,64,512]{2,1,0:T(8,128)} %slice.122), channel_id=1, source_target_pairs={{0,64},{2,66},{4,68},{6,70},{8,72},{10,74},{12,76},{14,78},{16,80}... | collective-permute-start | bytes 786440 | tf_op jit(solution)/shard_map/ppermute | solution.py:486
  7.3 11.7 %collective-permute-start.2 = (f32[2,16,512]{2,1,0:T(8,128)S(1)}, f32[2,16,512]{2,1,0:T(8,128)S(1)}, u32[]{:S(2)}, u32[]{:S(2)}) collective-permute-start(f32[2,16,512]{2,1,0:T(8,128)S(1)} %slice.160), channel_id=1, source_target_pairs={{0,65},{1,64},{2,67},{3,66},{4,69},{5,68},{6,71},{7,70},{8,73},{9,... | collective-permute-start | bytes 196616 | tf_op jit(solution)/shard_map/ppermute | solution.py:485
  24.6 1.4 %copy-start.1 = (f32[4608,128]{1,0:T(8,128)}, f32[4608,128]{1,0:T(8,128)S(1)}, u32[]{:S(2)}) copy-start(f32[4608,128]{1,0:T(8,128)S(1)} %source.1) | copy-start | bytes 7077892
  26.0 12.5 %copy-start.6 = (pred[128,256]{1,0:T(32,128)(4,1)S(1)}, pred[128,256]{1,0:T(32,128)(4,1)}, u32[]{:S(2)}) copy-start(pred[128,256]{1,0:T(32,128)(4,1)} %constant.120.clone) | copy-start | bytes 98308
  26.0 12.5 %copy-start.7 = (pred[128,256]{1,0:T(32,128)(4,1)S(1)}, pred[128,256]{1,0:T(32,128)(4,1)}, u32[]{:S(2)}) copy-start(pred[128,256]{1,0:T(32,128)(4,1)} %constant.119.clone) | copy-start | bytes 98308
  26.0 12.5 %copy-start.8 = (pred[128,256]{1,0:T(32,128)(4,1)S(1)}, pred[128,256]{1,0:T(32,128)(4,1)}, u32[]{:S(2)}) copy-start(pred[128,256]{1,0:T(32,128)(4,1)} %constant.118.clone) | copy-start | bytes 98308
  26.0 12.5 %copy-start.9 = (pred[128,256]{1,0:T(32,128)(4,1)S(1)}, pred[128,256]{1,0:T(32,128)(4,1)}, u32[]{:S(2)}) copy-start(pred[128,256]{1,0:T(32,128)(4,1)} %constant.117.clone) | copy-start | bytes 98308
  26.0 12.5 %copy-start.10 = (pred[128,256]{1,0:T(32,128)(4,1)S(1)}, pred[128,256]{1,0:T(32,128)(4,1)}, u32[]{:S(2)}) copy-start(pred[128,256]{1,0:T(32,128)(4,1)} %constant.116.clone) | copy-start | bytes 98308
  26.1 12.5 %copy-start.11 = (pred[128,256]{1,0:T(32,128)(4,1)S(1)}, pred[128,256]{1,0:T(32,128)(4,1)}, u32[]{:S(2)}) copy-start(pred[128,256]{1,0:T(32,128)(4,1)} %constant.115.clone) | copy-start | bytes 98308
  26.1 12.5 %copy-start.12 = (pred[128,256]{1,0:T(32,128)(4,1)S(1)}, pred[128,256]{1,0:T(32,128)(4,1)}, u32[]{:S(2)}) copy-start(pred[128,256]{1,0:T(32,128)(4,1)} %constant.114.clone) | copy-start | bytes 98308
  26.1 12.5 %copy-start.13 = (pred[128,256]{1,0:T(32,128)(4,1)S(1)}, pred[128,256]{1,0:T(32,128)(4,1)}, u32[]{:S(2)}) copy-start(pred[128,256]{1,0:T(32,128)(4,1)} %constant.113.clone) | copy-start | bytes 98308
  26.1 12.5 %copy-start.14 = (pred[128,256]{1,0:T(32,128)(4,1)S(1)}, pred[128,256]{1,0:T(32,128)(4,1)}, u32[]{:S(2)}) copy-start(pred[128,256]{1,0:T(32,128)(4,1)} %constant.112.clone) | copy-start | bytes 98308
  26.1 33.9 %copy-start.3 = (f32[2,64,66]{2,1,0:T(8,128)S(1)}, f32[2,64,66]{2,1,0:T(8,128)}, u32[]{:S(2)}) copy-start(f32[2,64,66]{2,1,0:T(8,128)} %constant.40.clone) | copy-start | bytes 101380
  26.1 33.9 %copy-start.5 = (f32[64,128]{1,0:T(8,128)S(1)}, f32[64,128]{1,0:T(8,128)}, u32[]{:S(2)}) copy-start(f32[64,128]{1,0:T(8,128)} %constant.87.clone) | copy-start | bytes 98308
  26.1 33.9 %copy-start.4 = (f32[66,128]{1,0:T(8,128)S(1)}, f32[66,128]{1,0:T(8,128)}, u32[]{:S(2)}) copy-start(f32[66,128]{1,0:T(8,128)} %constant.86.clone) | copy-start | bytes 101380
  26.1 42.2 %all-to-all-start = ((f32[64,72,128]{2,1,0:T(8,128)}), f32[64,72,128]{2,1,0:T(8,128)S(1)}, u32[]{:S(2)}, u32[]{:S(2)}) async-start(f32[64,72,128]{2,1,0:T(8,128)} %bitcast.43), calls=%async_computation | async-start | bytes 4718592 | tf_op jit(solution)/shard_map/all_to_all | solution.py:493
  37.0 31.4 %copy-start.2 = (bf16[1408,256]{1,0:T(8,128)(2,1)S(1)}, bf16[1408,256]{1,0:T(8,128)(2,1)}, u32[]{:S(2)}) copy-start(bf16[1408,256]{1,0:T(8,128)(2,1)} %constant.122.clone.weights) | copy-start | bytes 2162692

commit v2 on v1

--- a/solution.py
+++ b/solution.py
@@ -245,7 +245,7 @@
                 field[OUTER // 2 - LEFT + k, at, :] = mine[k]
         return carry
 
-    lax.fori_loop(0, half // 8, place, 0)
+    lax.fori_loop(0, half // 8, place, 0, unroll=2)
 
     def highpass(i, carry):
         both = jnp.concatenate([field[2 * i], field[2 * i + 1]], axis=1)
@@ -335,9 +335,8 @@
             outer_forward(*spot)
         for spot in spots:
             inner(spot[0], spot[4])
-        for spot in spots:
+        for j, spot in enumerate(spots):
             outer_backward(*spot)
-        for j in range(TOGETHER):
             for copy in copies(TOGETHER * i + j):
                 copy.start()
         return carry
@@ -408,7 +407,7 @@
 
 
 def hbm_spec():
-    return pl.BlockSpec(memory_space=pltpu.MemorySpace.HBM)
+    return pl.BlockSpec(memory_space=pl.ANY)
 
 
 def smem_spec():

time: 84 us -> 83 us (0.988)
  Pallas kernels: 21.3 us -> 20.3 us
    pallas_call x1, Pallas kernels: 15 us -> 14 us  [sinogram_side(): pl.pallas_call(sinogram_kernel, out_shape=jax.ShapeDtypeStruct((nproj, LE...]
where the time goes in v2:
time: 83 us; the launch traced here: 82.3 us
  other arithmetic  26.1 us (31%)
  Pallas kernels  20.3 us (24%)
  starting transfers between devices  15.5 us (19%)
  waiting for transfers between devices  15.3 us (18%)
  local copies, waits for them, and re-layouts  4.67 us (6%)
    select_n x1, other arithmetic, sinogram_side(): ends = jnp.where(tap_at == k, taps[0, k], ends)  21.4 us
    pallas_call x1, Pallas kernels, sinogram_side(): pl.pallas_call(sinogram_kernel, out_shape=jax.ShapeDtypeStruct((nproj, LE...  14 us
    all_to_all x1, starting transfers between devices, local(): lax.all_to_all(sent.reshape(rows, per * BLOCKS, LANES), 'ang', split_axis...  10.8 us
    all_to_all x1, waiting for transfers between devices, local(): lax.all_to_all(sent.reshape(rows, per * BLOCKS, LANES), 'ang', split_axis...  7.09 us
    ppermute x1, waiting for transfers between devices, local(): seam_halo = lax.ppermute(halo[:, :, :seam_cols], ('ang', 'row'), both)  4.62 us
    pallas_call x1, Pallas kernels, early_side(): pl.pallas_call(early_kernel, out_shape=shape, in_specs=[smem_spec(), smem...  4.32 us
    ppermute x1, starting transfers between devices, local(): halo = lax.ppermute(halo, 'row', across)  3.82 us
    ppermute x1, waiting for transfers between devices, local(): seam = lax.ppermute(projections[:, :, :seam_cols], 'ang', half_turn)  3.59 us
  transfers between devices with their start and end apart: 4, of which 3 were waited for; matrix products, arithmetic and copies ran while one was open for 34% of the time, Pallas kernels for 5%

profile of v2, /device:TPU:1, one launch (start us, length us, event | category | flops | bytes accessed | tf_op | source)
XLA Modules:
  0.0 82.3 jit_solution(1211677283839752379)
XLA Ops:
  0.0 0.0 copy-start
  0.0 1.4 %slice_select_fusion = f32[2,16,4096]{2,1,0:T(8,128)S(1)} fusion(f32[2,64,4096]{2,1,0:T(8,128)} %own.3, pred[]{:T(512)S(6)} %eq.3), kind=kLoop, calls=%fused_computation.1 | loop fusion | flops 131072 | bytes 1572865 | tf_op jit(solution)/shard_map/jit(_where)/select_n | solution.py:480
  1.4 3.8 %collective-permute-start = (f32[2,16,4096]{2,1,0:T(8,128)S(1)}, f32[2,16,4096]{2,1,0:T(8,128)S(1)}, u32[]{:S(2)}, u32[]{:S(2)}) collective-permute-start(f32[2,16,4096]{2,1,0:T(8,128)S(1)} %slice_select_fusion), channel_id=1, source_target_pairs={{0,1},{1,0},{2,3},{3,2},{4,5},{5,4},{6,7},{7,6},{8,9},{9,8},{10,11... | collective-permute-start | bytes 1572872 | tf_op jit(solution)/shard_map/ppermute | solution.py:486
  5.2 1.7 %slice.122 = f32[2,64,512]{2,1,0:T(8,128)} slice(f32[2,64,4096]{2,1,0:T(8,128)} %own.3), slice={[0:2], [0:64], [0:512]} | slice | bytes 524288 | tf_op jit(solution)/shard_map/slice | solution.py:485
  6.9 0.4 collective-permute-start.1
  7.3 0.5 collective-permute-start.2
  7.8 0.8 reduce_sum.9
  8.6 0.7 broadcast_divide_fusion.taps
  9.3 0.8 pad_add_fusion.ints
  10.1 0.0 copy-done
  10.1 4.3 %early.1 = f32[2,64,3840]{2,1,0:T(8,128)S(1)} custom-call(s32[5]{0:T(128)S(1)} %pad_add_fusion.ints, f32[2,33]{1,0:T(2,128)S(1)} %broadcast_divide_fusion.taps, f32[2,64,4096]{2,1,0:T(8,128)S(1)} %copy-done), custom_call_target="tpu_custom_call" | custom-call | flops 402653184 | bytes 4194304 | tf_op jit(solution)/shard_map/early/pallas_call | solution.py:420
  14.4 4.6 %collective-permute-done.2.seam_halo = f32[2,16,512]{2,1,0:T(8,128)S(1)} collective-permute-done((f32[2,16,512]{2,1,0:T(8,128)S(1)}, f32[2,16,512]{2,1,0:T(8,128)S(1)}, u32[]{:S(2)}, u32[]{:S(2)}) %collective-permute-start.2) | collective-permute-done | bytes 65568 | tf_op jit(solution)/shard_map/ppermute | solution.py:484
  19.0 3.6 %collective-permute-done.1.seam = f32[2,64,512]{2,1,0:T(8,128)S(1)} collective-permute-done((f32[2,64,512]{2,1,0:T(8,128)}, f32[2,64,512]{2,1,0:T(8,128)S(1)}, u32[]{:S(2)}, u32[]{:S(2)}) %collective-permute-start.1) | collective-permute-done | bytes 262176 | tf_op jit(solution)/shard_map/ppermute | solution.py:485
  22.6 0.0 collective-permute-done.halo
  22.6 2.0 %source.1 = f32[4608,128]{1,0:T(8,128)S(1)} custom-call(s32[5]{0:T(128)S(1)} %pad_add_fusion.ints, f32[2,33]{1,0:T(2,128)S(1)} %broadcast_divide_fusion.taps, f32[2,64,3840]{2,1,0:T(8,128)S(1)} %early.1, f32[2,64,4096]{2,1,0:T(8,128)S(1)} %copy-done, f32[2,16,4096]{2,1,0:T(8,128)S(1)} %collective-permute-done.halo, ...), custom_call_target="tpu_custom_call" | custom-call | tf_op jit(solution)/shard_map/source/pallas_call | solution.py:433
  24.6 0.0 copy-start.1
  24.6 1.4 %copy-done.1 = f32[4608,128]{1,0:T(8,128)} copy-done((f32[4608,128]{1,0:T(8,128)}, f32[4608,128]{1,0:T(8,128)S(1)}, u32[]{:S(2)}) %copy-start.1) | copy-done | bytes 2359320
  26.0 0.0 copy-start.6
  26.0 0.0 copy-start.7
  26.0 0.0 copy-start.8
  26.0 0.0 copy-start.9
  26.0 0.0 copy-start.10
  26.1 0.0 copy-start.11
  26.1 0.0 copy-start.12
  26.1 0.0 copy-start.13
  26.1 0.0 copy-start.14
  26.1 0.0 copy-start.3
  26.1 0.0 copy-start.5
  26.1 0.0 copy-start.4
  26.1 10.8 %all-to-all-start = ((f32[64,72,128]{2,1,0:T(8,128)}), f32[64,72,128]{2,1,0:T(8,128)S(1)}, u32[]{:S(2)}, u32[]{:S(2)}) async-start(f32[64,72,128]{2,1,0:T(8,128)} %bitcast.43), calls=%async_computation | async-start | bytes 4718592 | tf_op jit(solution)/shard_map/all_to_all | solution.py:492
  37.0 0.0 copy-start.2
  37.0 0.1 mul.13
  37.1 0.7 fusion.2
  37.8 0.7 fusion.1
  38.5 0.0 copy-done.6
  38.5 0.0 copy-done.7
  38.5 0.0 copy-done.8
  38.5 0.0 copy-done.9
  38.5 0.0 copy-done.10
  38.6 0.0 copy-done.11
  38.6 0.0 copy-done.12
  38.6 0.0 copy-done.13
  38.6 0.0 copy-done.14
  38.6 21.4 %select_select_fusion = f32[128,256]{1,0:T(8,128)S(1)} fusion(pred[128,256]{1,0:T(32,128)(4,1)S(1)} %copy-done.6, pred[128,256]{1,0:T(32,128)(4,1)S(1)} %copy-done.7, pred[128,256]{1,0:T(32,128)(4,1)S(1)} %copy-done.8, pred[128,256]{1,0:T(32,128)(4,1)S(1)} %copy-done.9, pred[128,256]{1,0:T(32,128)(4,1)S(1)} %copy-done.10, ...), kind=kLoop, calls=%fused_computation.3 | loop fusion | flops 1048576 | bytes 1179776 | tf_op jit(solution)/shard_map/jit(_where)/select_n | solution.py:452
  60.0 0.0 copy-done.3
  60.0 0.0 copy-done.5
  60.1 0.0 copy-done.4
  60.1 0.2 convolution_multiply_fusion
  60.3 1.0 %pad_maximum_fusion.table = f32[384,256]{1,0:T(8,128)S(1)} fusion(f32[128,256]{1,0:T(8,128)S(1)} %select_select_fusion, f32[192,256]{1,0:T(8,128)} %constant.121.clone, f32[64,128]{1,0:T(8,128)S(1)} %get-tuple-element.6, f32[64,128]{1,0:T(8,128)S(1)} %get-tuple-element.5), kind=kLoop, calls=%fused_computation.2 | loop fusion | flops 294912 | bytes 786432 | tf_op jit(solution)/shard_map/concatenate | solution.py:453
  61.2 7.1 %all-to-all-done = f32[64,72,128]{2,1,0:T(8,128)S(1)} async-done(((f32[64,72,128]{2,1,0:T(8,128)}), f32[64,72,128]{2,1,0:T(8,128)S(1)}, u32[]{:S(2)}, u32[]{:S(2)}) %all-to-all-start) | async-done | bytes 2359328 | tf_op jit(solution)/shard_map/all_to_all | solution.py:492
  68.3 0.0 copy-done.2
  68.3 14.0 %sinogram.1 = f32[128,8192]{1,0:T(8,128)} custom-call(f32[4608,128]{1,0:T(8,128)S(1)} %bitcast.42, f32[384,256]{1,0:T(8,128)S(1)} %pad_maximum_fusion.table, bf16[1408,256]{1,0:T(8,128)(2,1)S(1)} %copy-done.2), custom_call_target="tpu_custom_call" | custom-call | tf_op jit(solution)/shard_map/sinogram/pallas_call | solution.py:454
  (6 shorter events, 0.0 us)
Async XLA Ops:
  0.0 10.1 %copy-start = (f32[2,64,4096]{2,1,0:T(8,128)S(1)}, f32[2,64,4096]{2,1,0:T(8,128)}, u32[]{:S(2)}) copy-start(f32[2,64,4096]{2,1,0:T(8,128)} %own.3) | copy-start | bytes 6291460
  1.4 21.2 %collective-permute-start = (f32[2,16,4096]{2,1,0:T(8,128)S(1)}, f32[2,16,4096]{2,1,0:T(8,128)S(1)}, u32[]{:S(2)}, u32[]{:S(2)}) collective-permute-start(f32[2,16,4096]{2,1,0:T(8,128)S(1)} %slice_select_fusion), channel_id=1, source_target_pairs={{0,1},{1,0},{2,3},{3,2},{4,5},{5,4},{6,7},{7,6},{8,9},{9,8},{10,11... | collective-permute-start | bytes 1572872 | tf_op jit(solution)/shard_map/ppermute | solution.py:486
  6.9 15.7 %collective-permute-start.1 = (f32[2,64,512]{2,1,0:T(8,128)}, f32[2,64,512]{2,1,0:T(8,128)S(1)}, u32[]{:S(2)}, u32[]{:S(2)}) collective-permute-start(f32[2,64,512]{2,1,0:T(8,128)} %slice.122), channel_id=1, source_target_pairs={{0,64},{2,66},{4,68},{6,70},{8,72},{10,74},{12,76},{14,78},{16,80}... | collective-permute-start | bytes 786440 | tf_op jit(solution)/shard_map/ppermute | solution.py:485
  7.3 11.7 %collective-permute-start.2 = (f32[2,16,512]{2,1,0:T(8,128)S(1)}, f32[2,16,512]{2,1,0:T(8,128)S(1)}, u32[]{:S(2)}, u32[]{:S(2)}) collective-permute-start(f32[2,16,512]{2,1,0:T(8,128)S(1)} %slice.160), channel_id=1, source_target_pairs={{0,65},{1,64},{2,67},{3,66},{4,69},{5,68},{6,71},{7,70},{8,73},{9,... | collective-permute-start | bytes 196616 | tf_op jit(solution)/shard_map/ppermute | solution.py:484
  24.6 1.4 %copy-start.1 = (f32[4608,128]{1,0:T(8,128)}, f32[4608,128]{1,0:T(8,128)S(1)}, u32[]{:S(2)}) copy-start(f32[4608,128]{1,0:T(8,128)S(1)} %source.1) | copy-start | bytes 7077892
  26.0 12.5 %copy-start.6 = (pred[128,256]{1,0:T(32,128)(4,1)S(1)}, pred[128,256]{1,0:T(32,128)(4,1)}, u32[]{:S(2)}) copy-start(pred[128,256]{1,0:T(32,128)(4,1)} %constant.120.clone) | copy-start | bytes 98308
  26.0 12.5 %copy-start.7 = (pred[128,256]{1,0:T(32,128)(4,1)S(1)}, pred[128,256]{1,0:T(32,128)(4,1)}, u32[]{:S(2)}) copy-start(pred[128,256]{1,0:T(32,128)(4,1)} %constant.119.clone) | copy-start | bytes 98308
  26.0 12.5 %copy-start.8 = (pred[128,256]{1,0:T(32,128)(4,1)S(1)}, pred[128,256]{1,0:T(32,128)(4,1)}, u32[]{:S(2)}) copy-start(pred[128,256]{1,0:T(32,128)(4,1)} %constant.118.clone) | copy-start | bytes 98308
  26.0 12.5 %copy-start.9 = (pred[128,256]{1,0:T(32,128)(4,1)S(1)}, pred[128,256]{1,0:T(32,128)(4,1)}, u32[]{:S(2)}) copy-start(pred[128,256]{1,0:T(32,128)(4,1)} %constant.117.clone) | copy-start | bytes 98308
  26.0 12.5 %copy-start.10 = (pred[128,256]{1,0:T(32,128)(4,1)S(1)}, pred[128,256]{1,0:T(32,128)(4,1)}, u32[]{:S(2)}) copy-start(pred[128,256]{1,0:T(32,128)(4,1)} %constant.116.clone) | copy-start | bytes 98308
  26.1 12.5 %copy-start.11 = (pred[128,256]{1,0:T(32,128)(4,1)S(1)}, pred[128,256]{1,0:T(32,128)(4,1)}, u32[]{:S(2)}) copy-start(pred[128,256]{1,0:T(32,128)(4,1)} %constant.115.clone) | copy-start | bytes 98308
  26.1 12.5 %copy-start.12 = (pred[128,256]{1,0:T(32,128)(4,1)S(1)}, pred[128,256]{1,0:T(32,128)(4,1)}, u32[]{:S(2)}) copy-start(pred[128,256]{1,0:T(32,128)(4,1)} %constant.114.clone) | copy-start | bytes 98308
  26.1 12.5 %copy-start.13 = (pred[128,256]{1,0:T(32,128)(4,1)S(1)}, pred[128,256]{1,0:T(32,128)(4,1)}, u32[]{:S(2)}) copy-start(pred[128,256]{1,0:T(32,128)(4,1)} %constant.113.clone) | copy-start | bytes 98308
  26.1 12.5 %copy-start.14 = (pred[128,256]{1,0:T(32,128)(4,1)S(1)}, pred[128,256]{1,0:T(32,128)(4,1)}, u32[]{:S(2)}) copy-start(pred[128,256]{1,0:T(32,128)(4,1)} %constant.112.clone) | copy-start | bytes 98308
  26.1 33.9 %copy-start.3 = (f32[2,64,66]{2,1,0:T(8,128)S(1)}, f32[2,64,66]{2,1,0:T(8,128)}, u32[]{:S(2)}) copy-start(f32[2,64,66]{2,1,0:T(8,128)} %constant.40.clone) | copy-start | bytes 101380
  26.1 33.9 %copy-start.5 = (f32[64,128]{1,0:T(8,128)S(1)}, f32[64,128]{1,0:T(8,128)}, u32[]{:S(2)}) copy-start(f32[64,128]{1,0:T(8,128)} %constant.87.clone) | copy-start | bytes 98308
  26.1 33.9 %copy-start.4 = (f32[66,128]{1,0:T(8,128)S(1)}, f32[66,128]{1,0:T(8,128)}, u32[]{:S(2)}) copy-start(f32[66,128]{1,0:T(8,128)} %constant.86.clone) | copy-start | bytes 101380
  26.1 42.2 %all-to-all-start = ((f32[64,72,128]{2,1,0:T(8,128)}), f32[64,72,128]{2,1,0:T(8,128)S(1)}, u32[]{:S(2)}, u32[]{:S(2)}) async-start(f32[64,72,128]{2,1,0:T(8,128)} %bitcast.43), calls=%async_computation | async-start | bytes 4718592 | tf_op jit(solution)/shard_map/all_to_all | solution.py:492
  37.0 31.4 %copy-start.2 = (bf16[1408,256]{1,0:T(8,128)(2,1)S(1)}, bf16[1408,256]{1,0:T(8,128)(2,1)}, u32[]{:S(2)}) copy-start(bf16[1408,256]{1,0:T(8,128)(2,1)} %constant.122.clone.weights) | copy-start | bytes 2162692

commit v3 on v2

--- a/solution.py
+++ b/solution.py
@@ -292,8 +292,7 @@
             t_high = tail.astype(bf16).astype(f32)
             front = lax.broadcasted_iota(jnp.int32, (1, LANES), 1) < LANES // 2
             t_one = jnp.where(front, t_high, tail - t_high).astype(bf16)
-            t_two = jnp.where(front, t_high, 0.0).astype(bf16)
-            wrapped = mxu(jnp.concatenate([t_one, t_two], axis=1), end_w[...]).reshape(n, 8, 2 * LANES)
+            wrapped = mxu(jnp.concatenate([t_one, t_one], axis=1), end_w[...]).reshape(n, 8, 2 * LANES)
             g_re, g_im, r = gain_re[span][:, None, :], gain_im[span][:, None, :], ramp[span][:, None, :]
             re, im = times((spectrum[..., :LANES], spectrum[..., LANES:]), (g_re, g_im))
             re = re - r * wrapped[..., :LANES]

time: 83 us -> 83 us (level)
  no operation moved by 1% of the time
where the time goes in v3:
time: 83 us; the launch traced here: 82.3 us
  other arithmetic  26.1 us (31%)
  Pallas kernels  20.3 us (24%)
  starting transfers between devices  15.5 us (19%)
  waiting for transfers between devices  15.3 us (18%)
  local copies, waits for them, and re-layouts  4.67 us (6%)
    select_n x1, other arithmetic, sinogram_side(): ends = jnp.where(tap_at == k, taps[0, k], ends)  21.4 us
    pallas_call x1, Pallas kernels, sinogram_side(): pl.pallas_call(sinogram_kernel, out_shape=jax.ShapeDtypeStruct((nproj, LE...  14 us
    all_to_all x1, starting transfers between devices, local(): lax.all_to_all(sent.reshape(rows, per * BLOCKS, LANES), 'ang', split_axis...  10.8 us
    all_to_all x1, waiting for transfers between devices, local(): lax.all_to_all(sent.reshape(rows, per * BLOCKS, LANES), 'ang', split_axis...  7.09 us
    ppermute x1, waiting for transfers between devices, local(): seam_halo = lax.ppermute(halo[:, :, :seam_cols], ('ang', 'row'), both)  4.62 us
    pallas_call x1, Pallas kernels, early_side(): pl.pallas_call(early_kernel, out_shape=shape, in_specs=[smem_spec(), smem...  4.32 us
    ppermute x1, starting transfers between devices, local(): halo = lax.ppermute(halo, 'row', across)  3.82 us
    ppermute x1, waiting for transfers between devices, local(): seam = lax.ppermute(projections[:, :, :seam_cols], 'ang', half_turn)  3.59 us
  transfers between devices with their start and end apart: 4, of which 3 were waited for; matrix products, arithmetic and copies ran while one was open for 34% of the time, Pallas kernels for 5%

profile of v3, /device:TPU:1, one launch (start us, length us, event | category | flops | bytes accessed | tf_op | source)
XLA Modules:
  0.0 82.3 jit_solution(8268789403430615728)
XLA Ops:
  0.0 0.0 copy-start
  0.0 1.4 %slice_select_fusion = f32[2,16,4096]{2,1,0:T(8,128)S(1)} fusion(f32[2,64,4096]{2,1,0:T(8,128)} %own.3, pred[]{:T(512)S(6)} %eq.3), kind=kLoop, calls=%fused_computation.1 | loop fusion | flops 131072 | bytes 1572865 | tf_op jit(solution)/shard_map/jit(_where)/select_n | solution.py:479
  1.4 3.8 %collective-permute-start = (f32[2,16,4096]{2,1,0:T(8,128)S(1)}, f32[2,16,4096]{2,1,0:T(8,128)S(1)}, u32[]{:S(2)}, u32[]{:S(2)}) collective-permute-start(f32[2,16,4096]{2,1,0:T(8,128)S(1)} %slice_select_fusion), channel_id=1, source_target_pairs={{0,1},{1,0},{2,3},{3,2},{4,5},{5,4},{6,7},{7,6},{8,9},{9,8},{10,11... | collective-permute-start | bytes 1572872 | tf_op jit(solution)/shard_map/ppermute | solution.py:485
  5.2 1.7 %slice.122 = f32[2,64,512]{2,1,0:T(8,128)} slice(f32[2,64,4096]{2,1,0:T(8,128)} %own.3), slice={[0:2], [0:64], [0:512]} | slice | bytes 524288 | tf_op jit(solution)/shard_map/slice | solution.py:484
  6.9 0.4 collective-permute-start.1
  7.3 0.5 collective-permute-start.2
  7.8 0.8 reduce_sum.9
  8.6 0.7 broadcast_divide_fusion.taps
  9.3 0.8 pad_add_fusion.ints
  10.1 0.0 copy-done
  10.1 4.3 %early.1 = f32[2,64,3840]{2,1,0:T(8,128)S(1)} custom-call(s32[5]{0:T(128)S(1)} %pad_add_fusion.ints, f32[2,33]{1,0:T(2,128)S(1)} %broadcast_divide_fusion.taps, f32[2,64,4096]{2,1,0:T(8,128)S(1)} %copy-done), custom_call_target="tpu_custom_call" | custom-call | flops 402653184 | bytes 4194304 | tf_op jit(solution)/shard_map/early/pallas_call | solution.py:419
  14.4 4.6 %collective-permute-done.2.seam_halo = f32[2,16,512]{2,1,0:T(8,128)S(1)} collective-permute-done((f32[2,16,512]{2,1,0:T(8,128)S(1)}, f32[2,16,512]{2,1,0:T(8,128)S(1)}, u32[]{:S(2)}, u32[]{:S(2)}) %collective-permute-start.2) | collective-permute-done | bytes 65568 | tf_op jit(solution)/shard_map/ppermute | solution.py:483
  19.0 3.6 %collective-permute-done.1.seam = f32[2,64,512]{2,1,0:T(8,128)S(1)} collective-permute-done((f32[2,64,512]{2,1,0:T(8,128)}, f32[2,64,512]{2,1,0:T(8,128)S(1)}, u32[]{:S(2)}, u32[]{:S(2)}) %collective-permute-start.1) | collective-permute-done | bytes 262176 | tf_op jit(solution)/shard_map/ppermute | solution.py:484
  22.6 0.0 collective-permute-done.halo
  22.6 2.0 %source.1 = f32[4608,128]{1,0:T(8,128)S(1)} custom-call(s32[5]{0:T(128)S(1)} %pad_add_fusion.ints, f32[2,33]{1,0:T(2,128)S(1)} %broadcast_divide_fusion.taps, f32[2,64,3840]{2,1,0:T(8,128)S(1)} %early.1, f32[2,64,4096]{2,1,0:T(8,128)S(1)} %copy-done, f32[2,16,4096]{2,1,0:T(8,128)S(1)} %collective-permute-done.halo, ...), custom_call_target="tpu_custom_call" | custom-call | tf_op jit(solution)/shard_map/source/pallas_call | solution.py:432
  24.6 0.0 copy-start.1
  24.6 1.4 %copy-done.1 = f32[4608,128]{1,0:T(8,128)} copy-done((f32[4608,128]{1,0:T(8,128)}, f32[4608,128]{1,0:T(8,128)S(1)}, u32[]{:S(2)}) %copy-start.1) | copy-done | bytes 2359320
  26.0 0.0 copy-start.6
  26.0 0.0 copy-start.7
  26.0 0.0 copy-start.8
  26.0 0.0 copy-start.9
  26.0 0.0 copy-start.10
  26.0 0.0 copy-start.11
  26.1 0.0 copy-start.12
  26.1 0.0 copy-start.13
  26.1 0.0 copy-start.14
  26.1 0.0 copy-start.3
  26.1 0.0 copy-start.5
  26.1 0.0 copy-start.4
  26.1 10.8 %all-to-all-start = ((f32[64,72,128]{2,1,0:T(8,128)}), f32[64,72,128]{2,1,0:T(8,128)S(1)}, u32[]{:S(2)}, u32[]{:S(2)}) async-start(f32[64,72,128]{2,1,0:T(8,128)} %bitcast.43), calls=%async_computation | async-start | bytes 4718592 | tf_op jit(solution)/shard_map/all_to_all | solution.py:491
  37.0 0.0 copy-start.2
  37.0 0.1 mul.13
  37.1 0.7 fusion.2
  37.8 0.7 fusion.1
  38.5 0.0 copy-done.6
  38.5 0.0 copy-done.7
  38.5 0.0 copy-done.8
  38.5 0.0 copy-done.9
  38.5 0.0 copy-done.10
  38.5 0.0 copy-done.11
  38.6 0.0 copy-done.12
  38.6 0.0 copy-done.13
  38.6 0.0 copy-done.14
  38.6 21.4 %select_select_fusion = f32[128,256]{1,0:T(8,128)S(1)} fusion(pred[128,256]{1,0:T(32,128)(4,1)S(1)} %copy-done.6, pred[128,256]{1,0:T(32,128)(4,1)S(1)} %copy-done.7, pred[128,256]{1,0:T(32,128)(4,1)S(1)} %copy-done.8, pred[128,256]{1,0:T(32,128)(4,1)S(1)} %copy-done.9, pred[128,256]{1,0:T(32,128)(4,1)S(1)} %copy-done.10, ...), kind=kLoop, calls=%fused_computation.3 | loop fusion | flops 1048576 | bytes 1179776 | tf_op jit(solution)/shard_map/jit(_where)/select_n | solution.py:451
  60.0 0.0 copy-done.3
  60.0 0.0 copy-done.5
  60.0 0.0 copy-done.4
  60.1 0.2 convolution_multiply_fusion
  60.3 1.0 %pad_maximum_fusion.table = f32[384,256]{1,0:T(8,128)S(1)} fusion(f32[128,256]{1,0:T(8,128)S(1)} %select_select_fusion, f32[192,256]{1,0:T(8,128)} %constant.121.clone, f32[64,128]{1,0:T(8,128)S(1)} %get-tuple-element.6, f32[64,128]{1,0:T(8,128)S(1)} %get-tuple-element.5), kind=kLoop, calls=%fused_computation.2 | loop fusion | flops 294912 | bytes 786432 | tf_op jit(solution)/shard_map/concatenate | solution.py:452
  61.2 7.1 %all-to-all-done = f32[64,72,128]{2,1,0:T(8,128)S(1)} async-done(((f32[64,72,128]{2,1,0:T(8,128)}), f32[64,72,128]{2,1,0:T(8,128)S(1)}, u32[]{:S(2)}, u32[]{:S(2)}) %all-to-all-start) | async-done | bytes 2359328 | tf_op jit(solution)/shard_map/all_to_all | solution.py:491
  68.3 0.0 copy-done.2
  68.3 14.0 %sinogram.1 = f32[128,8192]{1,0:T(8,128)} custom-call(f32[4608,128]{1,0:T(8,128)S(1)} %bitcast.42, f32[384,256]{1,0:T(8,128)S(1)} %pad_maximum_fusion.table, bf16[1408,256]{1,0:T(8,128)(2,1)S(1)} %copy-done.2), custom_call_target="tpu_custom_call" | custom-call | tf_op jit(solution)/shard_map/sinogram/pallas_call | solution.py:453
  (6 shorter events, 0.0 us)
Async XLA Ops:
  0.0 10.1 %copy-start = (f32[2,64,4096]{2,1,0:T(8,128)S(1)}, f32[2,64,4096]{2,1,0:T(8,128)}, u32[]{:S(2)}) copy-start(f32[2,64,4096]{2,1,0:T(8,128)} %own.3) | copy-start | bytes 6291460
  1.4 21.2 %collective-permute-start = (f32[2,16,4096]{2,1,0:T(8,128)S(1)}, f32[2,16,4096]{2,1,0:T(8,128)S(1)}, u32[]{:S(2)}, u32[]{:S(2)}) collective-permute-start(f32[2,16,4096]{2,1,0:T(8,128)S(1)} %slice_select_fusion), channel_id=1, source_target_pairs={{0,1},{1,0},{2,3},{3,2},{4,5},{5,4},{6,7},{7,6},{8,9},{9,8},{10,11... | collective-permute-start | bytes 1572872 | tf_op jit(solution)/shard_map/ppermute | solution.py:485
  6.9 15.7 %collective-permute-start.1 = (f32[2,64,512]{2,1,0:T(8,128)}, f32[2,64,512]{2,1,0:T(8,128)S(1)}, u32[]{:S(2)}, u32[]{:S(2)}) collective-permute-start(f32[2,64,512]{2,1,0:T(8,128)} %slice.122), channel_id=1, source_target_pairs={{0,64},{2,66},{4,68},{6,70},{8,72},{10,74},{12,76},{14,78},{16,80}... | collective-permute-start | bytes 786440 | tf_op jit(solution)/shard_map/ppermute | solution.py:484
  7.3 11.7 %collective-permute-start.2 = (f32[2,16,512]{2,1,0:T(8,128)S(1)}, f32[2,16,512]{2,1,0:T(8,128)S(1)}, u32[]{:S(2)}, u32[]{:S(2)}) collective-permute-start(f32[2,16,512]{2,1,0:T(8,128)S(1)} %slice.160), channel_id=1, source_target_pairs={{0,65},{1,64},{2,67},{3,66},{4,69},{5,68},{6,71},{7,70},{8,73},{9,... | collective-permute-start | bytes 196616 | tf_op jit(solution)/shard_map/ppermute | solution.py:483
  24.6 1.4 %copy-start.1 = (f32[4608,128]{1,0:T(8,128)}, f32[4608,128]{1,0:T(8,128)S(1)}, u32[]{:S(2)}) copy-start(f32[4608,128]{1,0:T(8,128)S(1)} %source.1) | copy-start | bytes 7077892
  26.0 12.5 %copy-start.6 = (pred[128,256]{1,0:T(32,128)(4,1)S(1)}, pred[128,256]{1,0:T(32,128)(4,1)}, u32[]{:S(2)}) copy-start(pred[128,256]{1,0:T(32,128)(4,1)} %constant.120.clone) | copy-start | bytes 98308
  26.0 12.5 %copy-start.7 = (pred[128,256]{1,0:T(32,128)(4,1)S(1)}, pred[128,256]{1,0:T(32,128)(4,1)}, u32[]{:S(2)}) copy-start(pred[128,256]{1,0:T(32,128)(4,1)} %constant.119.clone) | copy-start | bytes 98308
  26.0 12.5 %copy-start.8 = (pred[128,256]{1,0:T(32,128)(4,1)S(1)}, pred[128,256]{1,0:T(32,128)(4,1)}, u32[]{:S(2)}) copy-start(pred[128,256]{1,0:T(32,128)(4,1)} %constant.118.clone) | copy-start | bytes 98308
  26.0 12.5 %copy-start.9 = (pred[128,256]{1,0:T(32,128)(4,1)S(1)}, pred[128,256]{1,0:T(32,128)(4,1)}, u32[]{:S(2)}) copy-start(pred[128,256]{1,0:T(32,128)(4,1)} %constant.117.clone) | copy-start | bytes 98308
  26.0 12.5 %copy-start.10 = (pred[128,256]{1,0:T(32,128)(4,1)S(1)}, pred[128,256]{1,0:T(32,128)(4,1)}, u32[]{:S(2)}) copy-start(pred[128,256]{1,0:T(32,128)(4,1)} %constant.116.clone) | copy-start | bytes 98308
  26.0 12.5 %copy-start.11 = (pred[128,256]{1,0:T(32,128)(4,1)S(1)}, pred[128,256]{1,0:T(32,128)(4,1)}, u32[]{:S(2)}) copy-start(pred[128,256]{1,0:T(32,128)(4,1)} %constant.115.clone) | copy-start | bytes 98308
  26.1 12.5 %copy-start.12 = (pred[128,256]{1,0:T(32,128)(4,1)S(1)}, pred[128,256]{1,0:T(32,128)(4,1)}, u32[]{:S(2)}) copy-start(pred[128,256]{1,0:T(32,128)(4,1)} %constant.114.clone) | copy-start | bytes 98308
  26.1 12.5 %copy-start.13 = (pred[128,256]{1,0:T(32,128)(4,1)S(1)}, pred[128,256]{1,0:T(32,128)(4,1)}, u32[]{:S(2)}) copy-start(pred[128,256]{1,0:T(32,128)(4,1)} %constant.113.clone) | copy-start | bytes 98308
  26.1 12.5 %copy-start.14 = (pred[128,256]{1,0:T(32,128)(4,1)S(1)}, pred[128,256]{1,0:T(32,128)(4,1)}, u32[]{:S(2)}) copy-start(pred[128,256]{1,0:T(32,128)(4,1)} %constant.112.clone) | copy-start | bytes 98308
  26.1 33.9 %copy-start.3 = (f32[2,64,66]{2,1,0:T(8,128)S(1)}, f32[2,64,66]{2,1,0:T(8,128)}, u32[]{:S(2)}) copy-start(f32[2,64,66]{2,1,0:T(8,128)} %constant.40.clone) | copy-start | bytes 101380
  26.1 33.9 %copy-start.5 = (f32[64,128]{1,0:T(8,128)S(1)}, f32[64,128]{1,0:T(8,128)}, u32[]{:S(2)}) copy-start(f32[64,128]{1,0:T(8,128)} %constant.87.clone) | copy-start | bytes 98308
  26.1 33.9 %copy-start.4 = (f32[66,128]{1,0:T(8,128)S(1)}, f32[66,128]{1,0:T(8,128)}, u32[]{:S(2)}) copy-start(f32[66,128]{1,0:T(8,128)} %constant.86.clone) | copy-start | bytes 101380
  26.1 42.2 %all-to-all-start = ((f32[64,72,128]{2,1,0:T(8,128)}), f32[64,72,128]{2,1,0:T(8,128)S(1)}, u32[]{:S(2)}, u32[]{:S(2)}) async-start(f32[64,72,128]{2,1,0:T(8,128)} %bitcast.43), calls=%async_computation | async-start | bytes 4718592 | tf_op jit(solution)/shard_map/all_to_all | solution.py:491
  37.0 31.4 %copy-start.2 = (bf16[1408,256]{1,0:T(8,128)(2,1)S(1)}, bf16[1408,256]{1,0:T(8,128)(2,1)}, u32[]{:S(2)}) copy-start(bf16[1408,256]{1,0:T(8,128)(2,1)} %constant.122.clone.weights) | copy-start | bytes 2162692

commit v4 on v3

--- a/solution.py
+++ b/solution.py
@@ -476,7 +476,7 @@
     nproj = per * ang
     seam_cols = LEFT * LANES
 
-    halo = jnp.where(here == 0, projections[:, rows - REACH :], projections[:, :REACH])
+    halo = lax.dynamic_slice_in_dim(projections, jnp.where(here == 0, rows - REACH, 0), REACH, axis=1)
     half_turn = [(i, (i + ang // 2) % ang) for i in range(ang)]
     across = [(i, 1 - i) for i in range(row)]
     both = [(a * row + r, b * row + s) for a, b in half_turn for r, s in across]

time: 83 us -> 82.8 us (level)
  local copies, waits for them, and re-layouts: 4.67 us -> 7.49 us
  waiting for transfers between devices: 15.3 us -> 13.5 us
  other arithmetic: 26.1 us -> 24.7 us
    ppermute x1, waiting for transfers between devices: 4.62 us -> 2.88 us  [local(): seam_halo = lax.ppermute(halo[:, :, :seam_cols], ('ang', 'row'), both)]
    unnamed x30 -> x32, local copies, waits for them, and re-layouts: 1.48 us -> 3.08 us
    select_n x1 -> x0, other arithmetic: 1.41 us -> none  [local(): jnp.where(here == 0, projections[:, rows - REACH:], projections[:, :REACH])]
    dynamic_slice x0 -> x1, local copies, waits for them, and re-layouts: none -> 1.08 us  [local(): lax.dynamic_slice_in_dim(projections, jnp.where(here == 0, rows - REACH,...]
    slice x1, local copies, waits for them, and re-layouts: 0.01 us -> 0.84 us  [local(): seam_halo = lax.ppermute(halo[:, :, :seam_cols], ('ang', 'row'), both)]
where the time goes in v4:
time: 82.8 us; the launch traced here: 82 us
  other arithmetic  24.7 us (30%)
  Pallas kernels  20.3 us (25%)
  starting transfers between devices  15.5 us (19%)
  waiting for transfers between devices  13.5 us (16%)
  local copies, waits for them, and re-layouts  7.49 us (9%)
    select_n x1, other arithmetic, sinogram_side(): ends = jnp.where(tap_at == k, taps[0, k], ends)  21.5 us
    pallas_call x1, Pallas kernels, sinogram_side(): pl.pallas_call(sinogram_kernel, out_shape=jax.ShapeDtypeStruct((nproj, LE...  14 us
    all_to_all x1, starting transfers between devices, local(): lax.all_to_all(sent.reshape(rows, per * BLOCKS, LANES), 'ang', split_axis...  10.8 us
    all_to_all x1, waiting for transfers between devices, local(): lax.all_to_all(sent.reshape(rows, per * BLOCKS, LANES), 'ang', split_axis...  7.02 us
    pallas_call x1, Pallas kernels, early_side(): pl.pallas_call(early_kernel, out_shape=shape, in_specs=[smem_spec(), smem...  4.33 us
    ppermute x1, starting transfers between devices, local(): halo = lax.ppermute(halo, 'row', across)  3.82 us
    ppermute x1, waiting for transfers between devices, local(): seam = lax.ppermute(projections[:, :, :seam_cols], 'ang', half_turn)  3.59 us
    unnamed x32, local copies, waits for them, and re-layouts  3.08 us
  transfers between devices with their start and end apart: 4, of which 3 were waited for; matrix products, arithmetic and copies ran while one was open for 34% of the time, Pallas kernels for 5%

profile of v4, /device:TPU:1, one launch (start us, length us, event | category | flops | bytes accessed | tf_op | source)
XLA Modules:
  0.0 82.0 jit_solution(8934495518541684903)
XLA Ops:
  0.0 1.1 %constant_dynamic-slice_fusion.1 = f32[2,16,4096]{2,1,0:T(8,128)S(1)} fusion(f32[2,64,4096]{2,1,0:T(8,128)} %own.3, s32[]{:T(128)S(6)} %select_n.105), kind=kLoop, calls=%fused_computation.7 | loop fusion | bytes 1048580 | tf_op jit(solution)/shard_map/dynamic_slice | solution.py:479
  1.1 3.8 %collective-permute-start = (f32[2,16,4096]{2,1,0:T(8,128)S(1)}, f32[2,16,4096]{2,1,0:T(8,128)S(1)}, u32[]{:S(2)}, u32[]{:S(2)}) collective-permute-start(f32[2,16,4096]{2,1,0:T(8,128)S(1)} %constant_dynamic-slice_fusion.1), channel_id=1, source_target_pairs={{0,1},{1,0},{2,3},{3,2},{4,5},{5,4},{6,7},{7,6},{8,9},{9,8},{10,11... | collective-permute-start | bytes 1572872 | tf_op jit(solution)/shard_map/ppermute | solution.py:485
  4.9 0.8 %constant_dynamic-slice_fusion = f32[2,16,512]{2,1,0:T(8,128)S(1)} fusion(f32[2,64,4096]{2,1,0:T(8,128)} %own.3, s32[]{:T(128)S(6)} %select_n.105), kind=kLoop, calls=%fused_computation.6 | loop fusion | bytes 131076 | tf_op jit(solution)/shard_map/slice | solution.py:483
  5.8 0.8 collective-permute-start.2
  6.5 1.0 %slice.114 = f32[2,64,512]{2,1,0:T(8,128)S(1)} slice(f32[2,64,4096]{2,1,0:T(8,128)} %own.3), slice={[0:2], [0:64], [0:512]} | slice | bytes 524288 | tf_op jit(solution)/shard_map/slice | solution.py:484
  7.5 0.1 collective-permute-start.1
  7.6 0.8 reduce_sum.9
  8.4 0.7 broadcast_divide_fusion.taps
  9.1 0.8 pad_add_fusion.ints
  9.9 0.0 copy-start
  9.9 1.6 %copy-done = f32[2,64,4096]{2,1,0:T(8,128)S(1)} copy-done((f32[2,64,4096]{2,1,0:T(8,128)S(1)}, f32[2,64,4096]{2,1,0:T(8,128)}, u32[]{:S(2)}) %copy-start) | copy-done | bytes 2097176
  11.5 4.3 %early.1 = f32[2,64,3840]{2,1,0:T(8,128)S(1)} custom-call(s32[5]{0:T(128)S(1)} %pad_add_fusion.ints, f32[2,33]{1,0:T(2,128)S(1)} %broadcast_divide_fusion.taps, f32[2,64,4096]{2,1,0:T(8,128)S(1)} %copy-done), custom_call_target="tpu_custom_call" | custom-call | flops 402653184 | bytes 4194304 | tf_op jit(solution)/shard_map/early/pallas_call | solution.py:419
  15.8 2.9 %collective-permute-done.2.seam_halo = f32[2,16,512]{2,1,0:T(8,128)S(1)} collective-permute-done((f32[2,16,512]{2,1,0:T(8,128)S(1)}, f32[2,16,512]{2,1,0:T(8,128)S(1)}, u32[]{:S(2)}, u32[]{:S(2)}) %collective-permute-start.2) | collective-permute-done | bytes 65568 | tf_op jit(solution)/shard_map/ppermute | solution.py:483
  18.7 3.6 %collective-permute-done.1.seam = f32[2,64,512]{2,1,0:T(8,128)S(1)} collective-permute-done((f32[2,64,512]{2,1,0:T(8,128)S(1)}, f32[2,64,512]{2,1,0:T(8,128)S(1)}, u32[]{:S(2)}, u32[]{:S(2)}) %collective-permute-start.1) | collective-permute-done | bytes 262176 | tf_op jit(solution)/shard_map/ppermute | solution.py:484
  22.3 0.0 collective-permute-done.halo
  22.3 2.0 %source.1 = f32[4608,128]{1,0:T(8,128)S(1)} custom-call(s32[5]{0:T(128)S(1)} %pad_add_fusion.ints, f32[2,33]{1,0:T(2,128)S(1)} %broadcast_divide_fusion.taps, f32[2,64,3840]{2,1,0:T(8,128)S(1)} %early.1, f32[2,64,4096]{2,1,0:T(8,128)S(1)} %copy-done, f32[2,16,4096]{2,1,0:T(8,128)S(1)} %collective-permute-done.halo, ...), custom_call_target="tpu_custom_call" | custom-call | tf_op jit(solution)/shard_map/source/pallas_call | solution.py:432
  24.3 0.0 copy-start.1
  24.3 1.4 %copy-done.1 = f32[4608,128]{1,0:T(8,128)} copy-done((f32[4608,128]{1,0:T(8,128)}, f32[4608,128]{1,0:T(8,128)S(1)}, u32[]{:S(2)}) %copy-start.1) | copy-done | bytes 2359320
  25.7 0.0 copy-start.6
  25.7 0.0 copy-start.7
  25.7 0.0 copy-start.8
  25.7 0.0 copy-start.9
  25.7 0.0 copy-start.10
  25.7 0.0 copy-start.11
  25.7 0.0 copy-start.12
  25.8 0.0 copy-start.13
  25.8 0.0 copy-start.14
  25.8 0.0 copy-start.15
  25.8 0.0 copy-start.3
  25.8 0.0 copy-start.5
  25.8 0.0 copy-start.4
  25.8 10.8 %all-to-all-start = ((f32[64,72,128]{2,1,0:T(8,128)}), f32[64,72,128]{2,1,0:T(8,128)S(1)}, u32[]{:S(2)}, u32[]{:S(2)}) async-start(f32[64,72,128]{2,1,0:T(8,128)} %bitcast.43), calls=%async_computation | async-start | bytes 4718592 | tf_op jit(solution)/shard_map/all_to_all | solution.py:491
  36.6 0.0 copy-start.2
  36.7 0.1 mul.13
  36.8 0.7 fusion.2
  37.4 0.7 fusion.1
  38.2 0.0 copy-done.6
  38.2 0.0 copy-done.7
  38.2 0.0 copy-done.8
  38.2 0.0 copy-done.9
  38.2 0.0 copy-done.10
  38.2 0.0 copy-done.11
  38.2 0.0 copy-done.12
  38.2 0.0 copy-done.13
  38.3 0.0 copy-done.14
  38.3 0.0 copy-done.15
  38.3 21.5 %select_select_fusion = f32[128,256]{1,0:T(8,128)S(1)} fusion(pred[128,256]{1,0:T(32,128)(4,1)S(1)} %copy-done.6, pred[128,256]{1,0:T(32,128)(4,1)S(1)} %copy-done.7, pred[128,256]{1,0:T(32,128)(4,1)S(1)} %copy-done.8, pred[128,256]{1,0:T(32,128)(4,1)S(1)} %copy-done.9, pred[128,256]{1,0:T(32,128)(4,1)S(1)} %copy-done.10, ...), kind=kLoop, calls=%fused_computation.2 | loop fusion | flops 1048576 | bytes 1179776 | tf_op jit(solution)/shard_map/jit(_where)/select_n | solution.py:451
  59.7 0.0 copy-done.3
  59.8 0.0 copy-done.5
  59.8 0.0 copy-done.4
  59.8 0.2 convolution_multiply_fusion
  60.0 1.0 %pad_maximum_fusion.table = f32[384,256]{1,0:T(8,128)S(1)} fusion(f32[128,256]{1,0:T(8,128)S(1)} %select_select_fusion, f32[192,256]{1,0:T(8,128)} %constant.125.clone, f32[64,128]{1,0:T(8,128)S(1)} %get-tuple-element.6, f32[64,128]{1,0:T(8,128)S(1)} %get-tuple-element.5), kind=kLoop, calls=%fused_computation.1 | loop fusion | flops 294912 | bytes 786432 | tf_op jit(solution)/shard_map/concatenate | solution.py:452
  61.0 7.0 %all-to-all-done = f32[64,72,128]{2,1,0:T(8,128)S(1)} async-done(((f32[64,72,128]{2,1,0:T(8,128)}), f32[64,72,128]{2,1,0:T(8,128)S(1)}, u32[]{:S(2)}, u32[]{:S(2)}) %all-to-all-start) | async-done | bytes 2359328 | tf_op jit(solution)/shard_map/all_to_all | solution.py:491
  68.0 0.0 copy-done.2
  68.0 14.0 %sinogram.1 = f32[128,8192]{1,0:T(8,128)} custom-call(f32[4608,128]{1,0:T(8,128)S(1)} %bitcast.42, f32[384,256]{1,0:T(8,128)S(1)} %pad_maximum_fusion.table, bf16[1408,256]{1,0:T(8,128)(2,1)S(1)} %copy-done.2), custom_call_target="tpu_custom_call" | custom-call | tf_op jit(solution)/shard_map/sinogram/pallas_call | solution.py:453
  (5 shorter events, 0.0 us)
Async XLA Ops:
  1.1 21.2 %collective-permute-start = (f32[2,16,4096]{2,1,0:T(8,128)S(1)}, f32[2,16,4096]{2,1,0:T(8,128)S(1)}, u32[]{:S(2)}, u32[]{:S(2)}) collective-permute-start(f32[2,16,4096]{2,1,0:T(8,128)S(1)} %constant_dynamic-slice_fusion.1), channel_id=1, source_target_pairs={{0,1},{1,0},{2,3},{3,2},{4,5},{5,4},{6,7},{7,6},{8,9},{9,8},{10,11... | collective-permute-start | bytes 1572872 | tf_op jit(solution)/shard_map/ppermute | solution.py:485
  5.8 12.9 %collective-permute-start.2 = (f32[2,16,512]{2,1,0:T(8,128)S(1)}, f32[2,16,512]{2,1,0:T(8,128)S(1)}, u32[]{:S(2)}, u32[]{:S(2)}) collective-permute-start(f32[2,16,512]{2,1,0:T(8,128)S(1)} %constant_dynamic-slice_fusion), channel_id=1, source_target_pairs={{0,65},{1,64},{2,67},{3,66},{4,69},{5,68},{6,71},{7,70},{8,73},{9,... | collective-permute-start | bytes 196616 | tf_op jit(solution)/shard_map/ppermute | solution.py:483
  7.5 14.8 %collective-permute-start.1 = (f32[2,64,512]{2,1,0:T(8,128)S(1)}, f32[2,64,512]{2,1,0:T(8,128)S(1)}, u32[]{:S(2)}, u32[]{:S(2)}) collective-permute-start(f32[2,64,512]{2,1,0:T(8,128)S(1)} %slice.114), channel_id=1, source_target_pairs={{0,64},{2,66},{4,68},{6,70},{8,72},{10,74},{12,76},{14,78},{16,80}... | collective-permute-start | bytes 786440 | tf_op jit(solution)/shard_map/ppermute | solution.py:484
  9.9 1.6 %copy-start = (f32[2,64,4096]{2,1,0:T(8,128)S(1)}, f32[2,64,4096]{2,1,0:T(8,128)}, u32[]{:S(2)}) copy-start(f32[2,64,4096]{2,1,0:T(8,128)} %own.3) | copy-start | bytes 6291460
  24.3 1.4 %copy-start.1 = (f32[4608,128]{1,0:T(8,128)}, f32[4608,128]{1,0:T(8,128)S(1)}, u32[]{:S(2)}) copy-start(f32[4608,128]{1,0:T(8,128)S(1)} %source.1) | copy-start | bytes 7077892
  25.7 12.5 %copy-start.6 = (pred[128,256]{1,0:T(32,128)(4,1)S(1)}, pred[128,256]{1,0:T(32,128)(4,1)}, u32[]{:S(2)}) copy-start(pred[128,256]{1,0:T(32,128)(4,1)} %constant.124.clone) | copy-start | bytes 98308
  25.7 12.5 %copy-start.7 = (pred[128,256]{1,0:T(32,128)(4,1)S(1)}, pred[128,256]{1,0:T(32,128)(4,1)}, u32[]{:S(2)}) copy-start(pred[128,256]{1,0:T(32,128)(4,1)} %constant.123.clone) | copy-start | bytes 98308
  25.7 12.5 %copy-start.8 = (pred[128,256]{1,0:T(32,128)(4,1)S(1)}, pred[128,256]{1,0:T(32,128)(4,1)}, u32[]{:S(2)}) copy-start(pred[128,256]{1,0:T(32,128)(4,1)} %constant.122.clone) | copy-start | bytes 98308
  25.7 12.5 %copy-start.9 = (pred[128,256]{1,0:T(32,128)(4,1)S(1)}, pred[128,256]{1,0:T(32,128)(4,1)}, u32[]{:S(2)}) copy-start(pred[128,256]{1,0:T(32,128)(4,1)} %constant.121.clone) | copy-start | bytes 98308
  25.7 12.5 %copy-start.10 = (pred[128,256]{1,0:T(32,128)(4,1)S(1)}, pred[128,256]{1,0:T(32,128)(4,1)}, u32[]{:S(2)}) copy-start(pred[128,256]{1,0:T(32,128)(4,1)} %constant.120.clone) | copy-start | bytes 98308
  25.7 12.5 %copy-start.11 = (pred[128,256]{1,0:T(32,128)(4,1)S(1)}, pred[128,256]{1,0:T(32,128)(4,1)}, u32[]{:S(2)}) copy-start(pred[128,256]{1,0:T(32,128)(4,1)} %constant.119.clone) | copy-start | bytes 98308
  25.7 12.5 %copy-start.12 = (pred[128,256]{1,0:T(32,128)(4,1)S(1)}, pred[128,256]{1,0:T(32,128)(4,1)}, u32[]{:S(2)}) copy-start(pred[128,256]{1,0:T(32,128)(4,1)} %constant.118.clone) | copy-start | bytes 98308
  25.8 12.5 %copy-start.13 = (pred[128,256]{1,0:T(32,128)(4,1)S(1)}, pred[128,256]{1,0:T(32,128)(4,1)}, u32[]{:S(2)}) copy-start(pred[128,256]{1,0:T(32,128)(4,1)} %constant.117.clone) | copy-start | bytes 98308
  25.8 12.5 %copy-start.14 = (pred[128,256]{1,0:T(32,128)(4,1)S(1)}, pred[128,256]{1,0:T(32,128)(4,1)}, u32[]{:S(2)}) copy-start(pred[128,256]{1,0:T(32,128)(4,1)} %constant.116.clone) | copy-start | bytes 98308
  25.8 12.5 %copy-start.15 = (pred[128,256]{1,0:T(32,128)(4,1)S(1)}, pred[128,256]{1,0:T(32,128)(4,1)}, u32[]{:S(2)}) copy-start(pred[128,256]{1,0:T(32,128)(4,1)} %constant.115.clone) | copy-start | bytes 98308
  25.8 33.9 %copy-start.3 = (f32[2,64,66]{2,1,0:T(8,128)S(1)}, f32[2,64,66]{2,1,0:T(8,128)}, u32[]{:S(2)}) copy-start(f32[2,64,66]{2,1,0:T(8,128)} %constant.41.clone) | copy-start | bytes 101380
  25.8 34.0 %copy-start.5 = (f32[64,128]{1,0:T(8,128)S(1)}, f32[64,128]{1,0:T(8,128)}, u32[]{:S(2)}) copy-start(f32[64,128]{1,0:T(8,128)} %constant.91.clone) | copy-start | bytes 98308
  25.8 34.0 %copy-start.4 = (f32[66,128]{1,0:T(8,128)S(1)}, f32[66,128]{1,0:T(8,128)}, u32[]{:S(2)}) copy-start(f32[66,128]{1,0:T(8,128)} %constant.90.clone) | copy-start | bytes 101380
  25.8 42.2 %all-to-all-start = ((f32[64,72,128]{2,1,0:T(8,128)}), f32[64,72,128]{2,1,0:T(8,128)S(1)}, u32[]{:S(2)}, u32[]{:S(2)}) async-start(f32[64,72,128]{2,1,0:T(8,128)} %bitcast.43), calls=%async_computation | async-start | bytes 4718592 | tf_op jit(solution)/shard_map/all_to_all | solution.py:491
  36.6 31.4 %copy-start.2 = (bf16[1408,256]{1,0:T(8,128)(2,1)S(1)}, bf16[1408,256]{1,0:T(8,128)(2,1)}, u32[]{:S(2)}) copy-start(bf16[1408,256]{1,0:T(8,128)(2,1)} %constant.126.clone.weights) | copy-start | bytes 2162692
